TPU v7x, 256 devices: a whole 4x4x8 slice. The times are simulated.
256 devices in a mesh: row: 16 (over x, y), col: 16 (over z, core).
Axes of the slice: x: 4, y: 4, z: 8, core: 2. Of those that a mesh axis runs over, the one named last changes fastest.
Arguments:
- momentum: float32 [7168, 18432], P('row', 'col'), may hold values from -100 to 100
- gradient: bfloat16 [7168, 18432], P('row', 'col'), may hold values from -6 to 6
- weight: float32 [7168, 18432], P('row', 'col'), may hold values from -6 to 6
- right_factor: float32 [256, 18432], P('row', 'col'), may hold values from -6 to 6
Outputs:
- new_momentum: float32 [7168, 18432], P('row', 'col')
- new_weight: float32 [7168, 18432], P('row', 'col')
- new_factor: float32 [256, 18432], P('row', 'col')
All inputs are finite; a program needn't handle non-finite values.
Results may differ from a plain program's by a relative error of at most 0.0003.
Values sent between devices are 32-bit elements; how exact they have to be, the bound alone decides.
No kernel may reach another device: no remote copies, remote signals or barrier semaphores. Data moves between devices by JAX's collectives and lax.ppermute only.
A program may use at most 64 MiB of HBM per device.

v0:
```python
import math

import jax
import jax.numpy as jnp
from jax import lax
from jax.sharding import PartitionSpec as P

MDIM = 7168
NDIM = 18432
RANK = 256


epsilon = 1e-06
momentum_keep = 0.95
learn_rate = 0.3
weight_decay = 0.1


def per_device(momentum, gradient, weight, right_factor):
    highest = lax.Precision.HIGHEST
    summed = momentum + gradient.astype(jnp.float32)
    band_rows = right_factor.shape[0]
    partial_value = lax.dot_general(
        summed,
        lax.all_gather(right_factor, "row", axis=0, tiled=True),
        (((1,), (1,)), ((), ())),
        precision=highest,
        preferred_element_type=jnp.float32,
    )
    projected = lax.psum(partial_value, "col")
    local_gram = lax.dot_general(
        projected,
        projected,
        (((0,), (0,)), ((), ())),
        precision=highest,
        preferred_element_type=jnp.float32,
    )
    gram_matrix = lax.psum(local_gram, "row")
    lower_factor = jnp.linalg.cholesky(gram_matrix)
    ortho = jax.scipy.linalg.solve_triangular(lower_factor, projected.T, lower=True).T
    step_scale = learn_rate * math.sqrt(MDIM / RANK)
    local_right = lax.dot_general(
        ortho,
        summed,
        (((0,), (0,)), ((), ())),
        precision=highest,
        preferred_element_type=jnp.float32,
    )
    right_product = lax.psum(local_right, "row")
    squares = lax.psum(jnp.sum(right_product * right_product, axis=1), "col")
    inverse = lax.rsqrt(squares / NDIM + epsilon)
    factor_all = right_product * inverse[:, None]
    momentum_delta = jnp.dot(
        ortho, right_product, precision=highest, preferred_element_type=jnp.float32
    )
    weight_delta = jnp.dot(ortho, factor_all, precision=highest, preferred_element_type=jnp.float32)
    new_factor = lax.dynamic_slice_in_dim(
        factor_all, lax.axis_index("row") * band_rows, band_rows, 0
    )
    new_momentum = summed - (1.0 - momentum_keep) * momentum_delta
    new_weight = (1.0 - learn_rate * weight_decay) * weight - step_scale * weight_delta
    return (new_momentum, new_weight, new_factor)


def solution(mesh):
    in_specs = (P("row", "col"), P("row", "col"), P("row", "col"), P("row", "col"))
    out_specs = (P("row", "col"), P("row", "col"), P("row", "col"))
    return jax.shard_map(
        per_device, mesh=mesh, in_specs=in_specs, out_specs=out_specs, check_vma=False
    )
```

profile of v0, /device:TPU:2, one launch (start us, length us, event | category | flops | bytes accessed | tf_op | source)
XLA Modules:
  0.0 486.4 jit_solution(14690274307144268185)
XLA Ops:
  7.2 0.0 all-gather.2.cloned.1.call-start
  7.2 0.7 all-gather.2.cloned.1.call-update
  7.9 0.0 all-reduce.5.cloned.1.call-start
  7.9 53.3 %all-gather.2.cloned.1.call-done = f32[256,1152]{1,0:T(8,128)} async-done(((f32[16,1152]{1,0:T(8,128)}), f32[256,1152]{1,0:T(8,128)}) %all-gather.2.cloned.1.call-update) | async-done | bytes 1179664 | tf_op jit(solution)/shard_map/all_gather | solution.py:25
  61.3 5.0 %fusion.3 = f32[448,256]{1,0:T(8,128)} fusion(f32[256,1152]{1,0:T(8,128)} %all-gather.2.cloned.1.call-done, f32[448,1152]{1,0:T(8,128)} %param.4, bf16[448,1152]{1,0:T(8,128)(2,1)} %param.5), kind=kOutput, calls=%fused_computation.11 | convolution fusion | flops 1586479104 | bytes 4734976 | tf_op jit(solution)/shard_map/dot_general | solution.py:23
  66.2 0.0 all-reduce.5.cloned.1.call-update
  66.3 0.0 all-reduce.7.cloned.1.call-start
  66.3 107.8 %all-reduce.5.cloned.1.call-done = f32[448,256]{1,0:T(8,128)} async-done(((f32[448,256]{1,0:T(8,128)}), f32[448,256]{1,0:T(8,128)}) %all-reduce.5.cloned.1.call-update) | async-done | bytes 458768 | tf_op jit(solution)/shard_map/psum | solution.py:30
  174.1 2.9 fusion.16
  177.0 0.0 all-reduce.7.cloned.1.call-update
  177.0 0.2 all-reduce.9.cloned.1.call-start
  177.3 94.1 %all-reduce.7.cloned.1.call-done = f32[256,256]{0,1:T(8,128)} async-done(((f32[256,256]{0,1:T(8,128)}), f32[256,256]{0,1:T(8,128)}) %all-reduce.7.cloned.1.call-update) | async-done | bytes 262160 | tf_op jit(solution)/shard_map/psum | solution.py:38
  271.3 1.1 copy.8
  272.4 1.0 fusion.4
  273.4 0.0 copy-start.6
  273.4 0.7 copy-done.6
  274.1 11.7 %cholesky.50 = f32[128,128]{1,0:T(8,128)S(1)} custom-call(f32[128,128]{1,0:T(8,128)S(1)} %cholesky.118), custom_call_target="Cholesky" | custom-call | tf_op jit(solution)/shard_map/jit(cholesky)/cholesky | solution.py:39
  285.9 0.0 copy-start
  285.9 0.0 copy-start.2
  285.9 9.8 %custom-call.15 = f32[1,128,128]{1,2,0:T(8,128)S(1)} custom-call(f32[1,128,128]{2,1,0:T(8,128)S(1)} %get-tuple-element.24), custom_call_target="InvertDiagBlocksLowerTriangular" | custom-call | tf_op jit(solution)/shard_map/jit(cholesky)/cholesky | solution.py:39
  295.7 1.0 constant_dynamic-update-slice_fusion
  296.8 1.1 convolution_subtract_fusion.1
  297.9 11.7 %cholesky.105 = f32[128,128]{1,0:T(8,128)S(1)} custom-call(f32[128,128]{1,0:T(8,128)S(1)} %convolution_subtract_fusion.1), custom_call_target="Cholesky" | custom-call | tf_op jit(solution)/shard_map/jit(cholesky)/cholesky | solution.py:39
  309.6 0.0 copy-start.5
  309.6 0.7 compare_reduce_fusion
  311.7 0.0 copy-done.5
  311.7 1.0 select_select_fusion
  312.7 0.1 triangular_solve.57
  312.8 5.5 %while.1 = (s32[]{:T(128)}, f32[256,256]{1,0:T(8,128)S(1)}, s32[2,2]{1,0:T(2,128)S(1)}, f32[2,128,128]{2,1,0:T(8,128)}, s32[]{:T(128)}) while((s32[]{:T(128)}, f32[256,256]{1,0:T(8,128)S(1)}, s32[2,2]{1,0:T(2,128)S(1)}, f32[2,128,128]{2,1,0:T(8,128)}, s32[]{:T(128)}) %tuple.27), condition=%wide.while_cond, body=%wide.while_body.sunk | while | flops 2 | bytes 132205 | solution.py:40
  313.0 0.6 fusion.27
  313.6 2.0 bitcast_dynamic-update-slice_fusion.2
  315.6 0.6 fusion.27
  316.2 2.0 bitcast_dynamic-update-slice_fusion.2
  318.2 0.0 copy-start.4
  318.3 20.5 %custom-call.16 = f32[2,128,128]{1,2,0:T(8,128)S(1)} custom-call(f32[2,128,128]{2,1,0:T(8,128)} %get-tuple-element.10), custom_call_target="InvertDiagBlocksLowerTriangular" | custom-call | tf_op jit(solution)/shard_map/jit(_solve_triangular)/triangular_solve | solution.py:40
  338.8 0.0 copy-done.4
  338.8 0.0 copy-start.7
  338.8 1.3 fusion.5
  340.1 0.0 copy-done.7
  340.1 1.3 convolution_subtract_fusion
  341.5 1.2 fusion.8
  342.7 0.0 copy-done
  342.7 0.0 copy-done.2
  342.7 3.4 fusion.2
  346.1 0.0 all-reduce.9.cloned.1.call-update
  346.1 96.6 %all-reduce.9.cloned.1.call-done = f32[256,1152]{1,0:T(8,128)} async-done(((f32[256,1152]{1,0:T(8,128)}), f32[256,1152]{1,0:T(8,128)}) %all-reduce.9.cloned.1.call-update) | async-done | bytes 1179664 | tf_op jit(solution)/shard_map/psum | solution.py:49
  442.7 2.0 multiply_reduce_fusion
  444.7 25.4 %psum.31 = f32[256]{0:T(256)} all-reduce(f32[256]{0:T(256)} %multiply_reduce_fusion), channel_id=1, replica_groups=mesh['row'=16,'col'=16] {'col'}, use_global_device_ids=true, to_apply=%region_8.9 | all-reduce | flops 256 | bytes 2048 | tf_op jit(solution)/shard_map/psum | solution.py:50
  470.1 0.0 copy-start.3
  470.1 0.8 add_rsqrt_fusion
  470.9 1.4 broadcast_multiply_fusion
  472.3 0.0 copy-done.3
  472.4 0.0 copy-start.1
  472.4 3.5 fusion
  475.9 0.6 constant_dynamic-slice_fusion.1
  476.5 0.0 copy-done.1
  476.5 3.4 fusion.1
  (8 shorter events, 0.1 us)
Async XLA Ops:
  7.2 54.1 %all-gather.2.cloned.1.call-start = ((), (), s32[]{:S(2)}) async-start(), calls=%async_computation | async-start | bytes 1253376 | tf_op jit(solution)/shard_map/all_gather | solution.py:25
  7.9 166.2 %all-reduce.5.cloned.1.call-start = ((), (), s32[]{:S(2)}) async-start(), calls=%async_computation.1 | async-start | bytes 917504 | tf_op jit(solution)/shard_map/psum | solution.py:30
  66.3 205.1 %all-reduce.7.cloned.1.call-start = ((), (), s32[]{:S(2)}) async-start(), calls=%async_computation.2 | async-start | bytes 524288 | tf_op jit(solution)/shard_map/psum | solution.py:38
  177.0 265.7 %all-reduce.9.cloned.1.call-start = ((), (), s32[]{:S(2)}) async-start(), calls=%async_computation.3 | async-start | bytes 2359296 | tf_op jit(solution)/shard_map/psum | solution.py:49
  273.4 0.7 copy-start.6
  285.9 56.8 %copy-start = (f32[448,1152]{1,0:T(8,128)S(1)}, f32[448,1152]{1,0:T(8,128)}, u32[]{:S(2)}) copy-start(f32[448,1152]{1,0:T(8,128)} %param.4) | copy-start | bytes 6193156
  285.9 56.8 %copy-start.2 = (bf16[448,1152]{1,0:T(8,128)(2,1)S(1)}, bf16[448,1152]{1,0:T(8,128)(2,1)}, u32[]{:S(2)}) copy-start(bf16[448,1152]{1,0:T(8,128)(2,1)} %param.5) | copy-start | bytes 3096580
  309.6 2.1 copy-start.5
  318.2 20.5 %copy-start.4 = (f32[256,256]{1,0:T(8,128)}, f32[256,256]{1,0:T(8,128)S(1)}, u32[]{:S(2)}) copy-start(f32[256,256]{1,0:T(8,128)S(1)} %get-tuple-element.83) | copy-start | bytes 786436
  338.8 1.3 copy-start.7
  470.1 2.3 copy-start.3
  472.4 4.2 copy-start.1
Sparse Core Ops, SparseCore 0:
  10.5 50.7 all-gather.1
  66.4 107.7 all-reduce.4
  178.2 93.0 all-reduce.6
  346.2 96.4 all-reduce.8
where the time goes:
time: 488 us; the launch traced here: 486 us
  waiting for transfers between devices  353 us (72%)
  other arithmetic  60.8 us (12%)
  blocking collectives  25.4 us (5%)
  matrix products  24 us (5%)
  between operations  15.3 us (3%)
  local copies, waits for them, and re-layouts  7.81 us (2%)
    psum x1, waiting for transfers between devices, per_device(): projected = lax.psum(partial_value, 'col')  108 us
    psum x1, waiting for transfers between devices, per_device(): right_product = lax.psum(local_right, 'row')  96.6 us
    psum x1, waiting for transfers between devices, per_device(): gram_matrix = lax.psum(local_gram, 'row')  94.1 us
    all_gather x1, waiting for transfers between devices, per_device(): lax.all_gather(right_factor, 'row', axis=0, tiled=True)  53.3 us
    another operation x6, other arithmetic, per_device(): lower_factor = jnp.linalg.cholesky(gram_matrix)  34 us
    psum x1, blocking collectives, per_device(): squares = lax.psum(jnp.sum(right_product * right_product, axis=1), 'col')  25.4 us
    another operation x3, other arithmetic, per_device(): jax.scipy.linalg.solve_triangular(lower_factor, projected.T, lower=True)  21.5 us
  transfers between devices with their start and end apart: 4, of which 4 were waited for; matrix products, arithmetic and copies ran while one was open for 0% of the time, Pallas kernels for 0%

commit v1 on v0

v1 whole, which is shorter than its diff:
```python
import math

import jax
import jax.numpy as jnp
from jax import lax
from jax.sharding import PartitionSpec as P

MDIM = 7168
NDIM = 18432
RANK = 256

epsilon = 1e-06
momentum_keep = 0.95
learn_rate = 0.3
weight_decay = 0.1

HIGHEST = lax.Precision.HIGHEST

ROWS = 16
DEPTH = 8
Z_GROUPS = [[2 * z + core for z in range(DEPTH)] for core in range(2)]
CORE_SWAP = [(i, i ^ 1) for i in range(2 * DEPTH)]


def z_pairs(partner):
    return [(2 * z + core, 2 * partner[z] + core) for z in range(DEPTH) for core in range(2)]


Z_BUTTERFLY = (
    z_pairs([1, 0, 3, 2, 5, 4, 7, 6]),
    z_pairs([7, 2, 1, 4, 3, 6, 5, 0]),
    z_pairs([3, 6, 5, 0, 7, 2, 1, 4]),
)


def product(a, b, contract):
    return lax.dot_general(
        a, b, (contract, ((), ())), precision=HIGHEST, preferred_element_type=jnp.float32
    )


def gather_over_row(block):
    copies = jnp.broadcast_to(block[None], (ROWS,) + block.shape)
    return lax.all_to_all(copies, "row", 0, 0).reshape((ROWS * block.shape[0],) + block.shape[1:])


def sum_over_row(whole):
    parts = whole.reshape((ROWS, whole.shape[0] // ROWS) + whole.shape[1:])
    return jnp.sum(lax.all_to_all(parts, "row", 0, 0), axis=0)


def sum_over_col(whole):
    core = lax.axis_index("col") % 2
    half = whole.shape[0] // 2
    kept = lax.dynamic_slice_in_dim(whole, core * half, half, 0)
    given = lax.dynamic_slice_in_dim(whole, (1 - core) * half, half, 0)
    chip = kept + lax.ppermute(given, "col", CORE_SWAP)
    parts = chip.reshape((DEPTH, half // DEPTH) + whole.shape[1:])
    part = jnp.sum(lax.all_to_all(parts, "col", 0, 0, axis_index_groups=Z_GROUPS), axis=0)
    copies = jnp.broadcast_to(part[None], (DEPTH,) + part.shape)
    mine = lax.all_to_all(copies, "col", 0, 0, axis_index_groups=Z_GROUPS).reshape(chip.shape)
    other = lax.ppermute(mine, "col", CORE_SWAP)
    return jnp.where(
        core == 0, jnp.concatenate([mine, other], 0), jnp.concatenate([other, mine], 0)
    )


def sum_small_over_col(value):
    value = value + lax.ppermute(value, "col", CORE_SWAP)
    for pairs in Z_BUTTERFLY:
        value = value + lax.ppermute(value, "col", pairs)
    return value


def per_device(momentum, gradient, weight, right_factor):
    summed = momentum + gradient.astype(jnp.float32)
    right_all = gather_over_row(right_factor)
    partial_value = product(right_all, summed, ((1,), (1,)))
    projected = sum_over_col(partial_value)
    local_gram = product(projected, projected, ((1,), (1,)))
    local_cross = product(projected, summed, ((1,), (0,)))
    both = gather_over_row(sum_over_row(jnp.concatenate([local_cross, local_gram], axis=1)))
    cross, gram_matrix = both[:, : summed.shape[1]], both[:, summed.shape[1] :]
    lower_factor = jnp.linalg.cholesky(gram_matrix)
    lower_inverse = jax.scipy.linalg.solve_triangular(
        lower_factor, jnp.eye(RANK, dtype=jnp.float32), lower=True
    )
    right_product = product(lower_inverse, cross, ((1,), (0,)))
    squares = sum_small_over_col(jnp.sum(right_product * right_product, axis=1)[None])[0]
    ortho_t = product(lower_inverse, projected, ((1,), (0,)))
    momentum_delta = product(ortho_t, right_product, ((0,), (0,)))
    new_momentum = summed - (1.0 - momentum_keep) * momentum_delta
    inverse = lax.rsqrt(squares / NDIM + epsilon)
    factor_all = right_product * inverse[:, None]
    weight_delta = product(ortho_t, factor_all, ((0,), (0,)))
    step_scale = learn_rate * math.sqrt(MDIM / RANK)
    band_rows = right_factor.shape[0]
    new_factor = lax.dynamic_slice_in_dim(
        factor_all, lax.axis_index("row") * band_rows, band_rows, 0
    )
    new_weight = (1.0 - learn_rate * weight_decay) * weight - step_scale * weight_delta
    return (new_momentum, new_weight, new_factor)


def solution(mesh):
    in_specs = (P("row", "col"), P("row", "col"), P("row", "col"), P("row", "col"))
    out_specs = (P("row", "col"), P("row", "col"), P("row", "col"))
    return jax.shard_map(
        per_device, mesh=mesh, in_specs=in_specs, out_specs=out_specs, check_vma=False
    )
```

time: 488 us -> 234 us (0.48)
  waiting for transfers between devices: 353 us -> 46.6 us
  blocking collectives: 25.4 us -> 59.6 us
  starting transfers between devices: 0.34 us -> 14.1 us
  between operations: 15.3 us -> 1.92 us
  local copies, waits for them, and re-layouts: 7.81 us -> 17.8 us
  other arithmetic: 60.8 us -> 67 us
    psum x3 -> x0, waiting for transfers between devices: 299 us -> none  [the longest x1 108 us: per_device(): projected = lax.psum(partial_value, 'col')]
    all_to_all x0 -> x3, blocking collectives: none -> 59.6 us  [the longest x1 25.4 us: sum_over_row(): return jnp.sum(lax.all_to_all(parts, 'row', 0, 0), axis=0)]
    all_gather x1 -> x0, waiting for transfers between devices: 53.3 us -> none  [per_device(): lax.all_gather(right_factor, 'row', axis=0, tiled=True)]
    all_to_all x0 -> x2, waiting for transfers between devices: none -> 34.8 us  [gather_over_row(): lax.all_to_all(copies, 'row', 0, 0)]
    psum x1 -> x0, blocking collectives: 25.4 us -> none  [per_device(): squares = lax.psum(jnp.sum(right_product * right_product, axis=1), 'col')]
    all_to_all x0 -> x2, starting transfers between devices: none -> 13.2 us  [gather_over_row(): lax.all_to_all(copies, 'row', 0, 0)]
    ppermute x0 -> x6, waiting for transfers between devices: none -> 11.9 us  [the longest x3 7.27 us: sum_small_over_col(): value = value + lax.ppermute(value, 'col', pairs)]
    another operation x6, other arithmetic: 34 us -> 41.3 us  [per_device(): lower_factor = jnp.linalg.cholesky(gram_matrix)]
  transfers between devices with their start and end apart: 4 -> 8, of which waited for: 4 -> 8; matrix products, arithmetic and copies ran while one was open for 0% -> 3% of each run, Pallas kernels for 0% -> 0%
where the time goes in v1:
time: 234 us; the launch traced here: 232 us
  other arithmetic  67 us (29%)
  blocking collectives  59.6 us (25%)
  waiting for transfers between devices  46.6 us (20%)
  matrix products  24.6 us (11%)
  local copies, waits for them, and re-layouts  17.8 us (8%)
  starting transfers between devices  14.1 us (6%)
    another operation x6, other arithmetic, per_device(): lower_factor = jnp.linalg.cholesky(gram_matrix)  41.3 us
    all_to_all x2, waiting for transfers between devices, gather_over_row(): lax.all_to_all(copies, 'row', 0, 0)  34.8 us
    all_to_all x1, blocking collectives, sum_over_row(): return jnp.sum(lax.all_to_all(parts, 'row', 0, 0), axis=0)  25.4 us
    another operation x3, other arithmetic, per_device(): jax.scipy.linalg.solve_triangular(lower_factor, jnp.eye(RANK, dtype=jnp.f...  21.5 us
    all_to_all x1, blocking collectives, sum_over_col(): lax.all_to_all(parts, 'col', 0, 0, axis_index_groups=Z_GROUPS)  20.6 us
    dot_general x7, matrix products, product(): lax.dot_general(a, b, (contract, ((), ())), precision=HIGHEST, preferred_...  20.3 us
    all_to_all x1, blocking collectives, sum_over_col(): lax.all_to_all(copies, 'col', 0, 0, axis_index_groups=Z_GROUPS)  13.5 us
    all_to_all x2, starting transfers between devices, gather_over_row(): lax.all_to_all(copies, 'row', 0, 0)  13.2 us
  transfers between devices with their start and end apart: 8, of which 8 were waited for; matrix products, arithmetic and copies ran while one was open for 3% of the time, Pallas kernels for 0%

profile of v1, /device:TPU:2, one launch (start us, length us, event | category | flops | bytes accessed | tf_op | source)
XLA Modules:
  0.0 231.7 jit_solution(2528814333078988300)
XLA Ops:
  0.6 0.0 copy-start.1
  0.6 2.1 broadcast_in_dim.9
  2.7 7.6 %all-to-all-start = ((f32[16,16,1152]{2,1,0:T(8,128)}), f32[16,16,1152]{2,1,0:T(8,128)}, u32[]{:S(2)}, u32[]{:S(2)}) async-start(f32[16,16,1152]{2,1,0:T(8,128)} %broadcast_in_dim.9), calls=%async_computation | async-start | bytes 2359296 | tf_op jit(solution)/shard_map/all_to_all | solution.py:44
  10.3 16.6 %all-to-all-done = f32[16,16,1152]{2,1,0:T(8,128)} async-done(((f32[16,16,1152]{2,1,0:T(8,128)}), f32[16,16,1152]{2,1,0:T(8,128)}, u32[]{:S(2)}, u32[]{:S(2)}) %all-to-all-start) | async-done | bytes 1179680 | tf_op jit(solution)/shard_map/all_to_all | solution.py:44
  26.9 3.3 %fusion.5 = f32[448,256]{1,0:T(8,128)S(1)} fusion(f32[256,1152]{1,0:T(8,128)} %bitcast, f32[448,1152]{1,0:T(8,128)S(1)} %copy-done, bf16[448,1152]{1,0:T(8,128)(2,1)S(1)} %copy-done.1), kind=kOutput, calls=%fused_computation.14 | convolution fusion | flops 1586479104 | bytes 4734976 | tf_op jit(solution)/shard_map/dot_general | solution.py:37
  30.2 0.7 dynamic-slice_bitcast_fusion
  30.9 0.0 collective-permute-start
  30.9 1.8 collective-permute-done
  32.7 1.6 bitcast_add_fusion.1
  34.4 1.8 copy.9
  36.1 20.6 %all_to_all.25 = f32[8,16,448]{2,1,0:T(8,128)S(1)} all-to-all(f32[8,16,448]{2,1,0:T(8,128)} %bitcast.55), channel_id=1, replica_groups={{0,2,4,6,8,10,12,14},{1,3,5,7,9,11,13,15},{16,18,20,22,24,26,28,30},{17..., dimensions={0} | all-to-all | bytes 458752 | tf_op jit(solution)/shard_map/all_to_all | solution.py:59
  56.8 13.5 %all_to_all.26 = f32[8,16,448]{2,1,0:T(8,128)S(1)} all-to-all(f32[8,16,448]{2,1,0:T(8,128)S(1)} %broadcast_in_dim.10), channel_id=1, replica_groups={{0,2,4,6,8,10,12,14},{1,3,5,7,9,11,13,15},{16,18,20,22,24,26,28,30},{17..., dimensions={0} | all-to-all | bytes 458752 | tf_op jit(solution)/shard_map/all_to_all | solution.py:61
  70.4 0.0 collective-permute-start.1
  70.4 1.7 collective-permute-done.1
  72.1 2.0 fusion.10
  74.0 3.4 %fusion.4 = f32[256,1152]{1,0:T(8,128)S(1)} fusion(f32[448,1152]{1,0:T(8,128)S(1)} %copy-done, bf16[448,1152]{1,0:T(8,128)(2,1)S(1)} %copy-done.1, f32[128,448]{1,0:T(8,128)} %collective-permute-done.1, f32[128,448]{1,0:T(8,128)S(1)} %bitcast.53, pred[]{:T(512)S(6)} %eq.10), kind=kOutput, calls=%fused_computation.13 | convolution fusion | flops 1586823168 | bytes 4734977 | tf_op jit(solution)/shard_map/dot_general | solution.py:37
  77.5 0.0 copy-done.5
  77.5 0.1 pad_maximum_fusion
  77.6 25.4 %all_to_all.27 = f32[16,16,1408]{2,1,0:T(8,128)S(1)} all-to-all(f32[16,16,1408]{2,1,0:T(8,128)S(1)} %bitcast.50), channel_id=1, replica_groups=mesh['row'=16,'col'=16] {'row'}, dimensions={0} | all-to-all | bytes 2883584 | tf_op jit(solution)/shard_map/all_to_all | solution.py:49
  103.0 0.7 reduce_sum.28
  103.7 2.1 broadcast_in_dim.11
  105.8 5.6 %all-to-all-start.4 = ((f32[16,16,1408]{2,1,0:T(8,128)}), f32[16,16,1408]{2,1,0:T(8,128)S(1)}, u32[]{:S(2)}, u32[]{:S(2)}) async-start(f32[16,16,1408]{2,1,0:T(8,128)} %broadcast_in_dim.11), calls=%async_computation.4 | async-start | bytes 2883584 | tf_op jit(solution)/shard_map/all_to_all | solution.py:44
  111.4 0.7 iota_compare_fusion
  112.1 18.2 %all-to-all-done.4 = f32[16,16,1408]{2,1,0:T(8,128)S(1)} async-done(((f32[16,16,1408]{2,1,0:T(8,128)}), f32[16,16,1408]{2,1,0:T(8,128)S(1)}, u32[]{:S(2)}, u32[]{:S(2)}) %all-to-all-start.4) | async-done | bytes 1441824 | tf_op jit(solution)/shard_map/all_to_all | solution.py:44
  130.2 0.8 slice.67
  131.0 1.8 copy.14
  132.8 1.0 fusion.6
  133.8 0.7 copy-done.6
  134.5 0.6 cholesky.118
  135.1 13.2 %cholesky.50 = f32[128,128]{1,0:T(8,128)} custom-call(f32[128,128]{1,0:T(8,128)} %cholesky.118), custom_call_target="Cholesky" | custom-call | tf_op jit(solution)/shard_map/jit(cholesky)/cholesky | solution.py:84
  148.3 1.6 cholesky.113
  149.8 1.5 select_reduce_fusion.1
  151.3 11.3 %custom-call.15 = f32[1,128,128]{1,2,0:T(8,128)} custom-call(f32[1,128,128]{2,1,0:T(8,128)} %get-tuple-element.24), custom_call_target="InvertDiagBlocksLowerTriangular" | custom-call | tf_op jit(solution)/shard_map/jit(cholesky)/cholesky | solution.py:84
  162.6 1.7 constant_dynamic-update-slice_fusion
  164.3 1.7 convolution_subtract_fusion.1
  166.0 0.0 copy-done.3
  166.0 13.2 %cholesky.105 = f32[128,128]{1,0:T(8,128)} custom-call(f32[128,128]{1,0:T(8,128)} %convolution_subtract_fusion.1), custom_call_target="Cholesky" | custom-call | tf_op jit(solution)/shard_map/jit(cholesky)/cholesky | solution.py:84
  179.2 1.5 select_reduce_fusion
  180.7 0.6 compare_reduce_fusion
  182.5 1.0 select_select_fusion
  183.5 0.1 triangular_solve.63
  183.6 5.0 %while.1 = (s32[]{:T(128)}, f32[256,256]{1,0:T(8,128)S(1)}, s32[2,2]{1,0:T(2,128)S(1)}, f32[2,128,128]{2,1,0:T(8,128)}, s32[]{:T(128)}) while((s32[]{:T(128)}, f32[256,256]{1,0:T(8,128)S(1)}, s32[2,2]{1,0:T(2,128)S(1)}, f32[2,128,128]{2,1,0:T(8,128)}, s32[]{:T(128)}) %tuple.28), condition=%wide.while_cond, body=%wide.while_body.sunk | while | flops 2 | bytes 132205 | solution.py:85
  183.6 0.6 fusion.31
  184.1 1.9 bitcast_dynamic-update-slice_fusion.2
  186.1 0.6 fusion.31
  186.7 1.9 bitcast_dynamic-update-slice_fusion.2
  188.6 20.5 %custom-call.16 = f32[2,128,128]{1,2,0:T(8,128)S(1)} custom-call(f32[2,128,128]{2,1,0:T(8,128)} %get-tuple-element.10), custom_call_target="InvertDiagBlocksLowerTriangular" | custom-call | tf_op jit(solution)/shard_map/jit(_solve_triangular)/triangular_solve | solution.py:85
  209.1 0.3 fusion.8
  209.4 0.3 convolution_subtract_fusion
  209.6 0.3 fusion.12
  209.9 2.6 %multiply_reduce_fusion = (f32[256]{0:T(256)S(1)}, f32[256,1152]{1,0:T(8,128)S(1)}) fusion(f32[256,1408]{1,0:T(8,128)} %bitcast.49, f32[128,256]{1,0:T(8,128)S(1)} %fusion.12, f32[128,256]{1,0:T(8,128)S(1)} %fusion.8), kind=kOutput, calls=%fused_computation.10 | convolution fusion | flops 906624768 | bytes 2622464 | tf_op jit(solution)/shard_map/dot_general | solution.py:37
  212.5 0.1 collective-permute-start.2
  212.6 1.1 collective-permute-done.2
  213.8 0.6 collective-permute-start.3
  214.3 3.0 %collective-permute-done.3 = f32[1,256]{1,0:T(1,128)S(1)} collective-permute-done((f32[1,256]{1,0:T(1,128)S(1)}, f32[1,256]{1,0:T(1,128)S(1)}, u32[]{:S(2)}, u32[]{:S(2)}) %collective-permute-start.3) | collective-permute-done | bytes 1056 | tf_op jit(solution)/shard_map/ppermute | solution.py:71
  217.3 0.0 collective-permute-start.4
  217.3 2.2 fusion.7
  219.5 2.6 %collective-permute-done.4 = f32[1,256]{1,0:T(1,128)S(1)} collective-permute-done((f32[1,256]{1,0:T(1,128)S(1)}, f32[1,256]{1,0:T(1,128)S(1)}, u32[]{:S(2)}, u32[]{:S(2)}) %collective-permute-start.4) | collective-permute-done | bytes 1056 | tf_op jit(solution)/shard_map/ppermute | solution.py:71
  222.1 0.2 collective-permute-start.5
  222.4 3.4 %fusion.1 = f32[448,1152]{1,0:T(8,128)} fusion(f32[256,448]{0,1:T(8,128)S(1)} %fusion.7, f32[256,1152]{1,0:T(8,128)S(1)} %get-tuple-element.28, f32[448,1152]{1,0:T(8,128)S(1)} %copy-done, bf16[448,1152]{1,0:T(8,128)(2,1)S(1)} %copy-done.2), kind=kOutput, calls=%fused_computation.5 | convolution fusion | flops 1587511296 | bytes 6799360 | tf_op jit(solution)/shard_map/dot_general | solution.py:37
  225.8 1.7 collective-permute-done.5
  227.5 0.1 broadcast_multiply_fusion
  227.7 3.4 %fusion = f32[448,1152]{1,0:T(8,128)} fusion(f32[256,448]{0,1:T(8,128)S(1)} %fusion.7, f32[256,1152]{1,0:T(8,128)S(1)} %broadcast_multiply_fusion, f32[448,1152]{1,0:T(8,128)S(1)} %copy-done.4), kind=kOutput, calls=%fused_computation.3 | convolution fusion | flops 1586995200 | bytes 5767168 | tf_op jit(solution)/shard_map/dot_general | solution.py:37
  231.1 0.6 constant_dynamic-slice_fusion.1
  (22 shorter events, 0.1 us)
Async XLA Ops:
  0.6 26.3 %copy-start.1 = (bf16[448,1152]{1,0:T(8,128)(2,1)S(1)}, bf16[448,1152]{1,0:T(8,128)(2,1)}, u32[]{:S(2)}) copy-start(bf16[448,1152]{1,0:T(8,128)(2,1)} %param.5) | copy-start | bytes 3096580
  2.7 24.2 %copy-start = (f32[448,1152]{1,0:T(8,128)S(1)}, f32[448,1152]{1,0:T(8,128)}, u32[]{:S(2)}) copy-start(f32[448,1152]{1,0:T(8,128)} %param.4) | copy-start | bytes 6193156
  2.7 24.2 %all-to-all-start = ((f32[16,16,1152]{2,1,0:T(8,128)}), f32[16,16,1152]{2,1,0:T(8,128)}, u32[]{:S(2)}, u32[]{:S(2)}) async-start(f32[16,16,1152]{2,1,0:T(8,128)} %broadcast_in_dim.9), calls=%async_computation | async-start | bytes 2359296 | tf_op jit(solution)/shard_map/all_to_all | solution.py:44
  30.9 1.8 collective-permute-start
  70.4 7.1 %copy-start.5 = (f32[8,16,448]{2,1,0:T(8,128)}, f32[8,16,448]{2,1,0:T(8,128)S(1)}, u32[]{:S(2)}) copy-start(f32[8,16,448]{2,1,0:T(8,128)S(1)} %all_to_all.26) | copy-start | bytes 688132
  70.4 1.7 collective-permute-start.1
  105.8 24.5 %all-to-all-start.4 = ((f32[16,16,1408]{2,1,0:T(8,128)}), f32[16,16,1408]{2,1,0:T(8,128)S(1)}, u32[]{:S(2)}, u32[]{:S(2)}) async-start(f32[16,16,1408]{2,1,0:T(8,128)} %broadcast_in_dim.11), calls=%async_computation.4 | async-start | bytes 2883584 | tf_op jit(solution)/shard_map/all_to_all | solution.py:44
  130.2 35.8 %copy-start.3 = (f32[16,16,1408]{2,1,0:T(8,128)}, f32[16,16,1408]{2,1,0:T(8,128)S(1)}, u32[]{:S(2)}) copy-start(f32[16,16,1408]{2,1,0:T(8,128)S(1)} %all-to-all-done.4) | copy-start | bytes 4325380
  133.8 0.7 copy-start.6
  179.2 29.8 %copy-start.7 = (pred[256,256]{1,0:T(32,128)(4,1)S(1)}, pred[256,256]{1,0:T(32,128)(4,1)}, u32[]{:S(2)}) copy-start(pred[256,256]{1,0:T(32,128)(4,1)} %iota_compare_fusion) | copy-start | bytes 196612
  212.5 1.2 collective-permute-start.2
  213.8 3.6 %collective-permute-start.3 = (f32[1,256]{1,0:T(1,128)S(1)}, f32[1,256]{1,0:T(1,128)S(1)}, u32[]{:S(2)}, u32[]{:S(2)}) collective-permute-start(f32[1,256]{1,0:T(1,128)S(1)} %add.71), channel_id=1, source_target_pairs={{0,2},{1,3},{2,0},{3,1},{4,6},{5,7},{6,4},{7,5},{8,10},{9,11},{10,... | collective-permute-start | bytes 3080 | tf_op jit(solution)/shard_map/ppermute | solution.py:71
  214.3 8.0 %copy-start.2 = (bf16[448,1152]{1,0:T(8,128)(2,1)S(1)}, bf16[448,1152]{1,0:T(8,128)(2,1)}, u32[]{:S(2)}) copy-start(bf16[448,1152]{1,0:T(8,128)(2,1)} %param.5) | copy-start | bytes 3096580
  217.3 4.8 %collective-permute-start.4 = (f32[1,256]{1,0:T(1,128)S(1)}, f32[1,256]{1,0:T(1,128)S(1)}, u32[]{:S(2)}, u32[]{:S(2)}) collective-permute-start(f32[1,256]{1,0:T(1,128)S(1)} %add.72), channel_id=1, source_target_pairs={{0,14},{1,15},{2,4},{3,5},{4,2},{5,3},{6,8},{7,9},{8,6},{9,7},{10,... | collective-permute-start | bytes 3080 | tf_op jit(solution)/shard_map/ppermute | solution.py:71
  222.1 5.4 %collective-permute-start.5 = (f32[1,256]{1,0:T(1,128)S(1)}, f32[1,256]{1,0:T(1,128)S(1)}, u32[]{:S(2)}, u32[]{:S(2)}) collective-permute-start(f32[1,256]{1,0:T(1,128)S(1)} %add.73), channel_id=1, source_target_pairs={{0,6},{1,7},{2,12},{3,13},{4,10},{5,11},{6,0},{7,1},{8,14},{9,15},... | collective-permute-start | bytes 3080 | tf_op jit(solution)/shard_map/ppermute | solution.py:71
  225.8 1.9 copy-start.4

commit v2 on v1

--- a/solution.py
+++ b/solution.py
@@ -3,6 +3,8 @@
 import jax
 import jax.numpy as jnp
 from jax import lax
+from jax.experimental import pallas as pl
+from jax.experimental.pallas import tpu as pltpu
 from jax.sharding import PartitionSpec as P
 
 MDIM = 7168
@@ -72,6 +74,91 @@
     return value
 
 
+BAND = 32
+SUB = 8
+LANES = 128
+
+
+def inverse_factor_kernel(gram_ref, out_ref, work):
+    n = out_ref.shape[0]
+    groups, tiles = BAND // SUB, n // LANES
+    row_of = lax.broadcasted_iota(jnp.int32, (SUB, LANES), 0)
+    work[...] = gram_ref[...]
+    for start in range(0, n, BAND):
+        columns = [
+            [
+                jnp.broadcast_to(
+                    work[start + SUB * g : start + SUB * (g + 1), start + j : start + j + 1],
+                    (SUB, LANES),
+                )
+                if g >= j // SUB
+                else None
+                for g in range(groups)
+            ]
+            for j in range(BAND)
+        ]
+        place = lax.broadcasted_iota(jnp.int32, (BAND, n), 1) - start
+        identity = (place == lax.broadcasted_iota(jnp.int32, (BAND, n), 0)).astype(jnp.float32)
+        band = jnp.where((place >= 0) & (place < BAND), identity, work[start : start + BAND, :])
+        rows = [
+            [band[SUB * g : SUB * (g + 1), LANES * t : LANES * (t + 1)] for t in range(tiles)]
+            for g in range(groups)
+        ]
+        for k in range(BAND):
+            own, at = divmod(k, SUB)
+            pivot = jnp.broadcast_to(columns[k][own][at : at + 1, :], (SUB, LANES))
+            root = lax.rsqrt(pivot)
+            reciprocal = root * root
+            for j in range(k + 1, BAND):
+                g0, at_j = divmod(j, SUB)
+                scale = jnp.broadcast_to(columns[k][g0][at_j : at_j + 1, :], (SUB, LANES)) * reciprocal
+                for g in range(g0, groups):
+                    columns[j][g] = columns[j][g] - columns[k][g] * scale
+            row = [jnp.broadcast_to(rows[own][t][at : at + 1, :], (SUB, LANES)) for t in range(tiles)]
+            scaled = [value * reciprocal for value in row]
+            for g in range(own, groups):
+                column = columns[k][g]
+                if g == own:
+                    column = jnp.where(row_of > at, column, 0.0)
+                for t in range(tiles):
+                    updated = rows[g][t] - column * scaled[t]
+                    if g == own:
+                        updated = jnp.where(row_of == at, row[t] * root, updated)
+                    rows[g][t] = updated
+        for g in range(groups):
+            for t in range(tiles):
+                work[start + SUB * g : start + SUB * (g + 1), LANES * t : LANES * (t + 1)] = rows[g][t]
+        below = n - start - BAND
+        if below:
+            update = lax.dot_general(
+                work[start : start + BAND, start + BAND :],
+                work[start : start + BAND, :],
+                (((0,), (0,)), ((), ())),
+                precision=HIGHEST,
+                preferred_element_type=jnp.float32,
+            )
+            place = lax.broadcasted_iota(jnp.int32, (below, n), 1) - start
+            old = jnp.where((place >= 0) & (place < BAND), 0.0, work[start + BAND :, :])
+            work[start + BAND :, :] = old - update
+    row = lax.broadcasted_iota(jnp.int32, (n, n), 0)
+    column = lax.broadcasted_iota(jnp.int32, (n, n), 1)
+    out_ref[...] = jnp.where(row >= column, work[...], 0.0)
+
+
+def inverse_factor(gram_and_more):
+    n = gram_and_more.shape[0]
+    block = pl.BlockSpec((n, n), lambda i: (0, 0))
+    return pl.pallas_call(
+        inverse_factor_kernel,
+        grid=(1,),
+        out_shape=jax.ShapeDtypeStruct((n, n), jnp.float32),
+        in_specs=[block],
+        out_specs=block,
+        scratch_shapes=[pltpu.VMEM((n, n), jnp.float32)],
+        cost_estimate=pl.CostEstimate(flops=2 * n**3, bytes_accessed=8 * n * n, transcendentals=n),
+    )(gram_and_more)
+
+
 def per_device(momentum, gradient, weight, right_factor):
     summed = momentum + gradient.astype(jnp.float32)
     right_all = gather_over_row(right_factor)
@@ -79,12 +166,9 @@
     projected = sum_over_col(partial_value)
     local_gram = product(projected, projected, ((1,), (1,)))
     local_cross = product(projected, summed, ((1,), (0,)))
-    both = gather_over_row(sum_over_row(jnp.concatenate([local_cross, local_gram], axis=1)))
-    cross, gram_matrix = both[:, : summed.shape[1]], both[:, summed.shape[1] :]
-    lower_factor = jnp.linalg.cholesky(gram_matrix)
-    lower_inverse = jax.scipy.linalg.solve_triangular(
-        lower_factor, jnp.eye(RANK, dtype=jnp.float32), lower=True
-    )
+    both = gather_over_row(sum_over_row(jnp.concatenate([local_gram, local_cross], axis=1)))
+    lower_inverse = inverse_factor(both)
+    cross = both[:, RANK:]
     right_product = product(lower_inverse, cross, ((1,), (0,)))
     squares = sum_small_over_col(jnp.sum(right_product * right_product, axis=1)[None])[0]
     ortho_t = product(lower_inverse, projected, ((1,), (0,)))

time: 234 us -> 163 us (0.70)
  other arithmetic: 67 us -> 2.64 us
  blocking collectives: 59.6 us -> 83.5 us
  waiting for transfers between devices: 46.6 us -> 27.3 us
  local copies, waits for them, and re-layouts: 17.8 us -> 7.07 us
  Pallas kernels: 0 us -> 9.93 us
  starting transfers between devices: 14.1 us -> 8.41 us
  matrix products: 24.6 us -> 22.2 us
    another operation x9 -> x0, other arithmetic: 62.8 us -> none  [the longest x6 41.3 us: per_device(): lower_factor = jnp.linalg.cholesky(gram_matrix)]
    all_to_all x0 -> x1, blocking collectives: none -> 23.9 us  [gather_over_row(): lax.all_to_all(copies, 'row', 0, 0)]
    all_to_all x2 -> x1, waiting for transfers between devices: 34.8 us -> 16.6 us  [gather_over_row(): lax.all_to_all(copies, 'row', 0, 0)]
    pallas_call x0 -> x1, Pallas kernels: none -> 9.93 us  [inverse_factor(): pl.pallas_call(inverse_factor_kernel, grid=(1,), out_shape=jax.ShapeDtype...]
    another operation x9 -> x0, local copies, waits for them, and re-layouts: 7.29 us -> none
    all_to_all x2 -> x1, starting transfers between devices: 13.2 us -> 7.61 us  [gather_over_row(): lax.all_to_all(copies, 'row', 0, 0)]
    another operation x5 -> x0, matrix products: 4.28 us -> none  [the longest x2 3.45 us: per_device(): lower_factor = jnp.linalg.cholesky(gram_matrix)]
  transfers between devices with their start and end apart: 8 -> 7, of which waited for: 8 -> 7; matrix products, arithmetic and copies ran while one was open for 3% -> 4% of each run, Pallas kernels for 0% -> 0%
where the time goes in v2:
time: 163 us; the launch traced here: 162 us
  blocking collectives  83.5 us (51%)
  waiting for transfers between devices  27.3 us (17%)
  matrix products  22.2 us (14%)
  Pallas kernels  9.93 us (6%)
  starting transfers between devices  8.41 us (5%)
  local copies, waits for them, and re-layouts  7.07 us (4%)
  other arithmetic  2.64 us (2%)
    all_to_all x1, blocking collectives, sum_over_row(): return jnp.sum(lax.all_to_all(parts, 'row', 0, 0), axis=0)  25.4 us
    all_to_all x1, blocking collectives, gather_over_row(): lax.all_to_all(copies, 'row', 0, 0)  23.9 us
    dot_general x7, matrix products, product(): lax.dot_general(a, b, (contract, ((), ())), precision=HIGHEST, preferred_...  22.2 us
    all_to_all x1, blocking collectives, sum_over_col(): lax.all_to_all(parts, 'col', 0, 0, axis_index_groups=Z_GROUPS)  20.6 us
    all_to_all x1, waiting for transfers between devices, gather_over_row(): lax.all_to_all(copies, 'row', 0, 0)  16.6 us
    all_to_all x1, blocking collectives, sum_over_col(): lax.all_to_all(copies, 'col', 0, 0, axis_index_groups=Z_GROUPS)  13.5 us
    pallas_call x1, Pallas kernels, inverse_factor(): pl.pallas_call(inverse_factor_kernel, grid=(1,), out_shape=jax.ShapeDtype...  9.93 us
    all_to_all x1, starting transfers between devices, gather_over_row(): lax.all_to_all(copies, 'row', 0, 0)  7.61 us
  transfers between devices with their start and end apart: 7, of which 7 were waited for; matrix products, arithmetic and copies ran while one was open for 4% of the time, Pallas kernels for 0%

profile of v2, /device:TPU:2, one launch (start us, length us, event | category | flops | bytes accessed | tf_op | source)
XLA Modules:
  0.0 161.7 jit_solution(6560091943485230515)
XLA Ops:
  0.6 0.0 copy-start.3
  0.6 2.1 %broadcast_in_dim.8 = f32[16,16,1152]{2,1,0:T(8,128)} broadcast(f32[16,1152]{1,0:T(8,128)} %param.7), dimensions={1,2} | broadcast | bytes 1253376 | tf_op jit(solution)/shard_map/broadcast_in_dim | solution.py:45
  2.7 0.0 copy-start
  2.7 7.6 %all-to-all-start = ((f32[16,16,1152]{2,1,0:T(8,128)}), f32[16,16,1152]{2,1,0:T(8,128)}, u32[]{:S(2)}, u32[]{:S(2)}) async-start(f32[16,16,1152]{2,1,0:T(8,128)} %broadcast_in_dim.8), calls=%async_computation | async-start | bytes 2359296 | tf_op jit(solution)/shard_map/all_to_all | solution.py:46
  10.3 16.6 %all-to-all-done = f32[16,16,1152]{2,1,0:T(8,128)} async-done(((f32[16,16,1152]{2,1,0:T(8,128)}), f32[16,16,1152]{2,1,0:T(8,128)}, u32[]{:S(2)}, u32[]{:S(2)}) %all-to-all-start) | async-done | bytes 1179680 | tf_op jit(solution)/shard_map/all_to_all | solution.py:46
  26.9 0.0 copy-done.3
  26.9 0.0 copy-done
  26.9 3.3 %fusion.5 = f32[448,256]{1,0:T(8,128)S(1)} fusion(f32[256,1152]{1,0:T(8,128)} %bitcast, f32[448,1152]{1,0:T(8,128)S(1)} %copy-done, bf16[448,1152]{1,0:T(8,128)(2,1)S(1)} %copy-done.3), kind=kOutput, calls=%fused_computation.10 | convolution fusion | flops 1586479104 | bytes 4734976 | tf_op jit(solution)/shard_map/dot_general | solution.py:39
  30.2 0.7 dynamic-slice_bitcast_fusion
  30.9 0.0 collective-permute-start
  30.9 1.8 %collective-permute-done = f32[128,448]{0,1:T(8,128)} collective-permute-done((f32[128,448]{0,1:T(8,128)}, f32[128,448]{0,1:T(8,128)}, u32[]{:S(2)}, u32[]{:S(2)}) %collective-permute-start) | collective-permute-done | bytes 229408 | tf_op jit(solution)/shard_map/ppermute | solution.py:59
  32.7 1.6 %bitcast_add_fusion = f32[128,448]{0,1:T(8,128)} fusion(f32[128,448]{0,1:T(8,128)} %collective-permute-done, f32[448,256]{1,0:T(8,128)S(1)} %fusion.5, s32[]{:T(128)S(6)} %select_n.26), kind=kLoop, calls=%fused_computation.13 | loop fusion | flops 57344 | bytes 688132 | tf_op jit(solution)/shard_map/add | solution.py:59
  34.4 1.8 %copy.8 = f32[128,448]{1,0:T(8,128)} copy(f32[128,448]{0,1:T(8,128)} %bitcast_add_fusion) | data formatting | bytes 458752 | tf_op jit(solution)/shard_map/add | solution.py:59
  36.1 20.6 %all_to_all.25 = f32[8,16,448]{2,1,0:T(8,128)S(1)} all-to-all(f32[8,16,448]{2,1,0:T(8,128)} %bitcast.25), channel_id=1, replica_groups={{0,2,4,6,8,10,12,14},{1,3,5,7,9,11,13,15},{16,18,20,22,24,26,28,30},{17..., dimensions={0} | all-to-all | bytes 458752 | tf_op jit(solution)/shard_map/all_to_all | solution.py:61
  56.8 13.5 %all_to_all.26 = f32[8,16,448]{2,1,0:T(8,128)S(1)} all-to-all(f32[8,16,448]{2,1,0:T(8,128)S(1)} %broadcast_in_dim.9), channel_id=1, replica_groups={{0,2,4,6,8,10,12,14},{1,3,5,7,9,11,13,15},{16,18,20,22,24,26,28,30},{17..., dimensions={0} | all-to-all | bytes 458752 | tf_op jit(solution)/shard_map/all_to_all | solution.py:63
  70.4 0.0 copy-start.4
  70.4 0.0 collective-permute-start.1
  70.4 1.7 %collective-permute-done.1 = f32[128,448]{1,0:T(8,128)} collective-permute-done((f32[128,448]{1,0:T(8,128)S(1)}, f32[128,448]{1,0:T(8,128)}, u32[]{:S(2)}, u32[]{:S(2)}) %collective-permute-start.1) | collective-permute-done | bytes 229408 | tf_op jit(solution)/shard_map/ppermute | solution.py:64
  72.1 3.4 %fusion.4 = f32[256,1152]{1,0:T(8,128)S(1)} fusion(f32[448,1152]{1,0:T(8,128)S(1)} %copy-done, bf16[448,1152]{1,0:T(8,128)(2,1)S(1)} %copy-done.3, f32[128,448]{1,0:T(8,128)} %collective-permute-done.1, f32[128,448]{1,0:T(8,128)S(1)} %bitcast.22, pred[]{:T(512)S(6)} %eq.5), kind=kOutput, calls=%fused_computation.9 | convolution fusion | flops 1586823168 | bytes 4734977 | tf_op jit(solution)/shard_map/dot_general | solution.py:39
  75.5 0.0 copy-done.4
  75.5 2.0 %fusion.7 = f32[256,256]{1,0:T(8,128)S(1)} fusion(f32[128,448]{1,0:T(8,128)} %collective-permute-done.1, f32[128,448]{1,0:T(8,128)S(1)} %bitcast.23, pred[]{:T(512)S(6)} %eq.5), kind=kOutput, calls=%fused_computation.16 | convolution fusion | flops 352665600 | bytes 720897 | tf_op jit(solution)/shard_map/dot_general | solution.py:39
  77.5 0.1 pad_maximum_fusion
  77.6 25.4 %all_to_all.27 = f32[16,16,1408]{2,1,0:T(8,128)S(1)} all-to-all(f32[16,16,1408]{2,1,0:T(8,128)S(1)} %bitcast.20), channel_id=1, replica_groups=mesh['row'=16,'col'=16] {'row'}, dimensions={0} | all-to-all | bytes 2883584 | tf_op jit(solution)/shard_map/all_to_all | solution.py:51
  103.0 0.7 reduce_sum.28
  103.7 1.0 broadcast_in_dim.10
  104.7 23.9 %all_to_all.28 = f32[16,16,1408]{2,1,0:T(8,128)} all-to-all(f32[16,16,1408]{2,1,0:T(8,128)S(1)} %broadcast_in_dim.10), channel_id=1, replica_groups=mesh['row'=16,'col'=16] {'row'}, dimensions={0} | all-to-all | bytes 2883584 | tf_op jit(solution)/shard_map/all_to_all | solution.py:46
  128.6 0.0 copy-start.1
  128.6 9.9 %shard_map.67 = f32[256,256]{1,0:T(8,128)} custom-call(f32[256,1408]{1,0:T(8,128)} %bitcast.18), custom_call_target="tpu_custom_call" | custom-call | flops 33554432 | bytes 524288 | tf_op jit(solution)/shard_map/pallas_call | solution.py:151
  138.5 0.0 copy-done.1
  138.5 3.2 %multiply_reduce_fusion = (f32[256]{0:T(256)S(1)}, f32[256,1152]{1,0:T(8,128)}) fusion(f32[256,256]{1,0:T(8,128)} %shard_map.67, f32[256,1408]{1,0:T(8,128)S(1)} %bitcast.19), kind=kOutput, calls=%fused_computation.8 | convolution fusion | flops 906559232 | bytes 2622464 | tf_op jit(solution)/shard_map/dot_general | solution.py:39
  141.7 0.0 copy-start.2
  141.7 0.0 collective-permute-start.2
  141.7 1.1 collective-permute-done.2
  142.9 0.6 collective-permute-start.3
  143.5 3.0 %collective-permute-done.3 = f32[1,256]{1,0:T(1,128)S(1)} collective-permute-done((f32[1,256]{1,0:T(1,128)S(1)}, f32[1,256]{1,0:T(1,128)S(1)}, u32[]{:S(2)}, u32[]{:S(2)}) %collective-permute-start.3) | collective-permute-done | bytes 1056 | tf_op jit(solution)/shard_map/ppermute | solution.py:73
  146.5 0.0 collective-permute-start.4
  146.5 2.2 %fusion.6 = f32[256,448]{0,1:T(8,128)S(1)} fusion(f32[256,256]{1,0:T(8,128)} %shard_map.67, f32[128,448]{1,0:T(8,128)} %collective-permute-done.1, f32[128,448]{1,0:T(8,128)} %bitcast.24, pred[]{:T(512)S(6)} %eq.5), kind=kOutput, calls=%fused_computation.15 | convolution fusion | flops 352665600 | bytes 1179649 | tf_op jit(solution)/shard_map/dot_general | solution.py:39
  148.7 2.5 %collective-permute-done.4 = f32[1,256]{1,0:T(1,128)S(1)} collective-permute-done((f32[1,256]{1,0:T(1,128)S(1)}, f32[1,256]{1,0:T(1,128)S(1)}, u32[]{:S(2)}, u32[]{:S(2)}) %collective-permute-start.4) | collective-permute-done | bytes 1056 | tf_op jit(solution)/shard_map/ppermute | solution.py:73
  151.2 0.2 collective-permute-start.5
  151.5 0.0 copy-done.2
  151.5 4.6 %fusion.1 = f32[448,1152]{1,0:T(8,128)} fusion(f32[256,448]{0,1:T(8,128)S(1)} %fusion.6, f32[256,1152]{1,0:T(8,128)S(1)} %copy-done.2, f32[448,1152]{1,0:T(8,128)S(1)} %copy-done, bf16[448,1152]{1,0:T(8,128)(2,1)} %param.5), kind=kOutput, calls=%fused_computation.3 | convolution fusion | flops 1587511296 | bytes 6799360 | tf_op jit(solution)/shard_map/dot_general | solution.py:39
  156.1 0.0 copy-start.5
  156.1 0.5 collective-permute-done.5
  156.6 0.1 broadcast_multiply_fusion
  156.8 0.9 copy-done.5
  157.6 3.4 %fusion = f32[448,1152]{1,0:T(8,128)} fusion(f32[256,448]{0,1:T(8,128)S(1)} %fusion.6, f32[256,1152]{1,0:T(8,128)S(1)} %broadcast_multiply_fusion, f32[448,1152]{1,0:T(8,128)S(1)} %copy-done.5), kind=kOutput, calls=%fused_computation.1 | convolution fusion | flops 1586995200 | bytes 5767168 | tf_op jit(solution)/shard_map/dot_general | solution.py:39
  161.1 0.6 constant_dynamic-slice_fusion
  (6 shorter events, 0.1 us)
Async XLA Ops:
  0.6 26.3 %copy-start.3 = (bf16[448,1152]{1,0:T(8,128)(2,1)S(1)}, bf16[448,1152]{1,0:T(8,128)(2,1)}, u32[]{:S(2)}) copy-start(bf16[448,1152]{1,0:T(8,128)(2,1)} %param.5) | copy-start | bytes 3096580
  2.7 24.2 %copy-start = (f32[448,1152]{1,0:T(8,128)S(1)}, f32[448,1152]{1,0:T(8,128)}, u32[]{:S(2)}) copy-start(f32[448,1152]{1,0:T(8,128)} %param.4) | copy-start | bytes 6193156
  2.7 24.2 %all-to-all-start = ((f32[16,16,1152]{2,1,0:T(8,128)}), f32[16,16,1152]{2,1,0:T(8,128)}, u32[]{:S(2)}, u32[]{:S(2)}) async-start(f32[16,16,1152]{2,1,0:T(8,128)} %broadcast_in_dim.8), calls=%async_computation | async-start | bytes 2359296 | tf_op jit(solution)/shard_map/all_to_all | solution.py:46
  30.9 1.8 %collective-permute-start = (f32[128,448]{0,1:T(8,128)}, f32[128,448]{0,1:T(8,128)}, u32[]{:S(2)}, u32[]{:S(2)}) collective-permute-start(f32[128,448]{0,1:T(8,128)} %dynamic-slice_bitcast_fusion), channel_id=1, source_target_pairs={{0,1},{1,0},{2,3},{3,2},{4,5},{5,4},{6,7},{7,6},{8,9},{9,8},{10,11... | collective-permute-start | bytes 688136 | tf_op jit(solution)/shard_map/ppermute | solution.py:59
  70.4 5.1 %copy-start.4 = (f32[8,16,448]{2,1,0:T(8,128)}, f32[8,16,448]{2,1,0:T(8,128)S(1)}, u32[]{:S(2)}) copy-start(f32[8,16,448]{2,1,0:T(8,128)S(1)} %all_to_all.26) | copy-start | bytes 688132
  70.4 1.7 %collective-permute-start.1 = (f32[128,448]{1,0:T(8,128)S(1)}, f32[128,448]{1,0:T(8,128)}, u32[]{:S(2)}, u32[]{:S(2)}) collective-permute-start(f32[128,448]{1,0:T(8,128)S(1)} %bitcast.21), channel_id=1, source_target_pairs={{0,1},{1,0},{2,3},{3,2},{4,5},{5,4},{6,7},{7,6},{8,9},{9,8},{10,11... | collective-permute-start | bytes 688136 | tf_op jit(solution)/shard_map/ppermute | solution.py:64
  128.6 9.9 %copy-start.1 = (f32[16,16,1408]{2,1,0:T(8,128)S(1)}, f32[16,16,1408]{2,1,0:T(8,128)}, u32[]{:S(2)}) copy-start(f32[16,16,1408]{2,1,0:T(8,128)} %all_to_all.28) | copy-start | bytes 4325380
  141.7 9.7 %copy-start.2 = (f32[256,1152]{1,0:T(8,128)S(1)}, f32[256,1152]{1,0:T(8,128)}, u32[]{:S(2)}) copy-start(f32[256,1152]{1,0:T(8,128)} %get-tuple-element.4) | copy-start | bytes 3538948
  141.7 1.1 collective-permute-start.2
  142.9 3.6 %collective-permute-start.3 = (f32[1,256]{1,0:T(1,128)S(1)}, f32[1,256]{1,0:T(1,128)S(1)}, u32[]{:S(2)}, u32[]{:S(2)}) collective-permute-start(f32[1,256]{1,0:T(1,128)S(1)} %add.47), channel_id=1, source_target_pairs={{0,2},{1,3},{2,0},{3,1},{4,6},{5,7},{6,4},{7,5},{8,10},{9,11},{10,... | collective-permute-start | bytes 3080 | tf_op jit(solution)/shard_map/ppermute | solution.py:73
  146.5 4.8 %collective-permute-start.4 = (f32[1,256]{1,0:T(1,128)S(1)}, f32[1,256]{1,0:T(1,128)S(1)}, u32[]{:S(2)}, u32[]{:S(2)}) collective-permute-start(f32[1,256]{1,0:T(1,128)S(1)} %add.48), channel_id=1, source_target_pairs={{0,14},{1,15},{2,4},{3,5},{4,2},{5,3},{6,8},{7,9},{8,6},{9,7},{10,... | collective-permute-start | bytes 3080 | tf_op jit(solution)/shard_map/ppermute | solution.py:73
  151.2 5.4 %collective-permute-start.5 = (f32[1,256]{1,0:T(1,128)S(1)}, f32[1,256]{1,0:T(1,128)S(1)}, u32[]{:S(2)}, u32[]{:S(2)}) collective-permute-start(f32[1,256]{1,0:T(1,128)S(1)} %add.49), channel_id=1, source_target_pairs={{0,6},{1,7},{2,12},{3,13},{4,10},{5,11},{6,0},{7,1},{8,14},{9,15},... | collective-permute-start | bytes 3080 | tf_op jit(solution)/shard_map/ppermute | solution.py:73
  156.1 1.6 copy-start.5

commit v3 on v2

--- a/solution.py
+++ b/solution.py
@@ -24,8 +24,12 @@
 CORE_SWAP = [(i, i ^ 1) for i in range(2 * DEPTH)]
 
 
+def pairs_on(partner, others, index):
+    return [(index(i, j), index(partner[i], j)) for i in range(len(partner)) for j in range(others)]
+
+
 def z_pairs(partner):
-    return [(2 * z + core, 2 * partner[z] + core) for z in range(DEPTH) for core in range(2)]
+    return pairs_on(partner, 2, lambda z, core: 2 * z + core)
 
 
 Z_BUTTERFLY = (
@@ -34,10 +38,9 @@
     z_pairs([3, 6, 5, 0, 7, 2, 1, 4]),
 )
 
-
-def product(a, b, contract):
+def product(a, b, contract, precision=HIGHEST):
     return lax.dot_general(
-        a, b, (contract, ((), ())), precision=HIGHEST, preferred_element_type=jnp.float32
+        a, b, (contract, ((), ())), precision=precision, preferred_element_type=jnp.float32
     )
 
 
@@ -53,18 +56,36 @@
 
 def sum_over_col(whole):
     core = lax.axis_index("col") % 2
-    half = whole.shape[0] // 2
-    kept = lax.dynamic_slice_in_dim(whole, core * half, half, 0)
-    given = lax.dynamic_slice_in_dim(whole, (1 - core) * half, half, 0)
+    rows, columns = whole.shape
+    half = columns // 2
+    kept = lax.dynamic_slice_in_dim(whole, core * half, half, 1)
+    given = lax.dynamic_slice_in_dim(whole, (1 - core) * half, half, 1)
     chip = kept + lax.ppermute(given, "col", CORE_SWAP)
-    parts = chip.reshape((DEPTH, half // DEPTH) + whole.shape[1:])
+    parts = chip.reshape(DEPTH, rows // DEPTH, half)
     part = jnp.sum(lax.all_to_all(parts, "col", 0, 0, axis_index_groups=Z_GROUPS), axis=0)
     copies = jnp.broadcast_to(part[None], (DEPTH,) + part.shape)
     mine = lax.all_to_all(copies, "col", 0, 0, axis_index_groups=Z_GROUPS).reshape(chip.shape)
-    other = lax.ppermute(mine, "col", CORE_SWAP)
+    return in_order(core == 0, mine, lax.ppermute(mine, "col", CORE_SWAP), 1)
+
+
+def in_order(first, mine, other, axis=0):
     return jnp.where(
-        core == 0, jnp.concatenate([mine, other], 0), jnp.concatenate([other, mine], 0)
-    )
+        first, jnp.concatenate([mine, other], axis), jnp.concatenate([other, mine], axis)
+    )
+
+
+def band_index():
+    place = lax.axis_index("col")
+    return place % 2 * 4 + place // 2 % 4
+
+
+def gather_bands(band, other):
+    place = lax.axis_index("col")
+    core, z = place % 2, place // 2
+    received, other = lax.optimization_barrier((lax.ppermute(band, "col", Z_BUTTERFLY[0]), other))
+    mine = in_order(z % 2 == 0, band, received)
+    mine = in_order(z // 2 % 2 == 0, mine, lax.ppermute(mine, "col", Z_BUTTERFLY[1]))
+    return in_order(core == 0, mine, lax.ppermute(mine, "col", CORE_SWAP)), other
 
 
 def sum_small_over_col(value):
@@ -162,21 +183,31 @@
 def per_device(momentum, gradient, weight, right_factor):
     summed = momentum + gradient.astype(jnp.float32)
     right_all = gather_over_row(right_factor)
-    partial_value = product(right_all, summed, ((1,), (1,)))
-    projected = sum_over_col(partial_value)
-    local_gram = product(projected, projected, ((1,), (1,)))
-    local_cross = product(projected, summed, ((1,), (0,)))
-    both = gather_over_row(sum_over_row(jnp.concatenate([local_gram, local_cross], axis=1)))
-    lower_inverse = inverse_factor(both)
-    cross = both[:, RANK:]
+    projected = sum_over_col(product(summed, right_all, ((1,), (1,))))
+    local_cross = product(projected, summed, ((0,), (0,)))
+    local_gram = product(projected, projected, ((0,), (0,)))
+    rows, band = RANK // ROWS, RANK // 8
+    at = band_index() * band
+    band_parts = [lax.dynamic_slice_in_dim(local_gram, at + i, rows, 0) for i in range(0, band, rows)]
+    bands = jnp.broadcast_to(jnp.concatenate(band_parts, 1)[None], (ROWS, rows, RANK * band // rows))
+    parts = jnp.concatenate([local_cross.reshape(ROWS, rows, -1), bands], axis=2)
+    taken = lax.all_to_all(parts, "row", 0, 0)
+    columns = summed.shape[1]
+    gram_band = jnp.sum(taken[:, :, columns:], axis=0)
+    gram_band = jnp.concatenate(
+        [gram_band[:, i * RANK : (i + 1) * RANK] for i in range(band // rows)], 0
+    )
+    gram_matrix, cross_part = gather_bands(gram_band, jnp.sum(taken[:, :, :columns], axis=0))
+    cross = gather_over_row(cross_part)
+    lower_inverse = inverse_factor(gram_matrix)
     right_product = product(lower_inverse, cross, ((1,), (0,)))
     squares = sum_small_over_col(jnp.sum(right_product * right_product, axis=1)[None])[0]
-    ortho_t = product(lower_inverse, projected, ((1,), (0,)))
-    momentum_delta = product(ortho_t, right_product, ((0,), (0,)))
+    ortho = product(projected, lower_inverse, ((1,), (1,)))
+    momentum_delta = product(ortho, right_product, ((1,), (0,)), lax.Precision.HIGH)
     new_momentum = summed - (1.0 - momentum_keep) * momentum_delta
     inverse = lax.rsqrt(squares / NDIM + epsilon)
     factor_all = right_product * inverse[:, None]
-    weight_delta = product(ortho_t, factor_all, ((0,), (0,)))
+    weight_delta = product(ortho, factor_all, ((1,), (0,)), lax.Precision.HIGH)
     step_scale = learn_rate * math.sqrt(MDIM / RANK)
     band_rows = right_factor.shape[0]
     new_factor = lax.dynamic_slice_in_dim(

time: 163 us -> 150 us (0.920)
  blocking collectives: 83.5 us -> 61.1 us
  waiting for transfers between devices: 27.3 us -> 39.1 us
  starting transfers between devices: 8.41 us -> 15 us
  matrix products: 22.2 us -> 16.3 us
    all_to_all x2 -> x1, blocking collectives: 49.3 us -> 28.8 us  [per_device(): taken = lax.all_to_all(parts, 'row', 0, 0)]
    ppermute x1 -> x4, waiting for transfers between devices: 1.66 us -> 11.2 us  [the longest x1 5.02 us: gather_bands(): lax.ppermute(mine, 'col', Z_BUTTERFLY[1])]
    dot_general x7, matrix products: 22.2 us -> 16.3 us  [product(): lax.dot_general(a, b, (contract, ((), ())), precision=precision, preferre...]
    all_to_all x1 -> x2, starting transfers between devices: 7.61 us -> 12.5 us  [gather_over_row(): lax.all_to_all(copies, 'row', 0, 0)]
    ppermute x3, waiting for transfers between devices: 6.07 us -> 8.49 us  [sum_small_over_col(): value = value + lax.ppermute(value, 'col', pairs)]
    add x1 -> x0, local copies, waits for them, and re-layouts: 1.77 us -> none  [sum_over_col(): chip = kept + lax.ppermute(given, 'col', CORE_SWAP)]
    all_to_all x1 -> x2, waiting for transfers between devices: 16.6 us -> 16.6 us  [gather_over_row(): lax.all_to_all(copies, 'row', 0, 0)]
  transfers between devices with their start and end apart: 7 -> 11, of which waited for: 7 -> 10; matrix products, arithmetic and copies ran while one was open for 4% -> 3% of each run, Pallas kernels for 0% -> 7%
where the time goes in v3:
time: 150 us
  blocking collectives  61.1 us (41%)
  waiting for transfers between devices  39.1 us (26%)
  matrix products  16.3 us (11%)
  starting transfers between devices  15 us (10%)
  Pallas kernels  9.82 us (7%)
  local copies, waits for them, and re-layouts  5.69 us (4%)
  other arithmetic  2.1 us (1%)
    all_to_all x1, blocking collectives, per_device(): taken = lax.all_to_all(parts, 'row', 0, 0)  28.8 us
    all_to_all x1, blocking collectives, sum_over_col(): lax.all_to_all(parts, 'col', 0, 0, axis_index_groups=Z_GROUPS)  19.7 us
    all_to_all x2, waiting for transfers between devices, gather_over_row(): lax.all_to_all(copies, 'row', 0, 0)  16.6 us
    dot_general x7, matrix products, product(): lax.dot_general(a, b, (contract, ((), ())), precision=precision, preferre...  16.3 us
    all_to_all x1, blocking collectives, sum_over_col(): lax.all_to_all(copies, 'col', 0, 0, axis_index_groups=Z_GROUPS)  12.6 us
    all_to_all x2, starting transfers between devices, gather_over_row(): lax.all_to_all(copies, 'row', 0, 0)  12.5 us
    pallas_call x1, Pallas kernels, inverse_factor(): pl.pallas_call(inverse_factor_kernel, grid=(1,), out_shape=jax.ShapeDtype...  9.82 us
    ppermute x3, waiting for transfers between devices, sum_small_over_col(): value = value + lax.ppermute(value, 'col', pairs)  8.49 us
  transfers between devices with their start and end apart: 11, of which 10 were waited for; matrix products, arithmetic and copies ran while one was open for 3% of the time, Pallas kernels for 7%

profile of v3, /device:TPU:2, one launch (start us, length us, event | category | flops | bytes accessed | tf_op | source)
XLA Modules:
  0.0 149.9 jit_solution(4842517364846189698)
XLA Ops:
  0.6 0.0 copy-start
  0.6 0.0 copy-start.1
  0.7 2.1 %broadcast_in_dim.10 = f32[16,16,1152]{2,1,0:T(8,128)} broadcast(f32[16,1152]{1,0:T(8,128)} %param.7), dimensions={1,2} | broadcast | bytes 1253376 | tf_op jit(solution)/shard_map/broadcast_in_dim | solution.py:48
  2.8 7.5 %all-to-all-start = ((f32[16,16,1152]{2,1,0:T(8,128)}), f32[16,16,1152]{2,1,0:T(8,128)}, u32[]{:S(2)}, u32[]{:S(2)}) async-start(f32[16,16,1152]{2,1,0:T(8,128)} %broadcast_in_dim.10), calls=%async_computation | async-start | bytes 2359296 | tf_op jit(solution)/shard_map/all_to_all | solution.py:49
  10.3 16.6 %all-to-all-done = f32[16,16,1152]{2,1,0:T(8,128)} async-done(((f32[16,16,1152]{2,1,0:T(8,128)}), f32[16,16,1152]{2,1,0:T(8,128)}, u32[]{:S(2)}, u32[]{:S(2)}) %all-to-all-start) | async-done | bytes 1179680 | tf_op jit(solution)/shard_map/all_to_all | solution.py:49
  26.8 0.0 copy-done
  26.8 0.0 copy-done.1
  26.8 3.3 %fusion.3 = f32[448,256]{1,0:T(8,128)S(1)} fusion(f32[256,1152]{1,0:T(8,128)} %bitcast, f32[448,1152]{1,0:T(8,128)S(1)} %copy-done, bf16[448,1152]{1,0:T(8,128)(2,1)S(1)} %copy-done.1), kind=kOutput, calls=%fused_computation.9 | convolution fusion | flops 1586479104 | bytes 4734976 | tf_op jit(solution)/shard_map/dot_general | solution.py:42
  30.1 0.7 constant_dynamic-slice_fusion.3
  30.8 0.0 collective-permute-start
  30.8 1.8 %collective-permute-done = f32[448,128]{1,0:T(8,128)} collective-permute-done((f32[448,128]{1,0:T(8,128)}, f32[448,128]{1,0:T(8,128)}, u32[]{:S(2)}, u32[]{:S(2)}) %collective-permute-start) | collective-permute-done | bytes 229408 | tf_op jit(solution)/shard_map/ppermute | solution.py:63
  32.7 1.0 dynamic-slice_add_fusion
  33.6 19.7 %all_to_all.25 = f32[8,56,128]{2,1,0:T(8,128)S(1)} all-to-all(f32[8,56,128]{2,1,0:T(8,128)S(1)} %bitcast.21), channel_id=1, replica_groups={{0,2,4,6,8,10,12,14},{1,3,5,7,9,11,13,15},{16,18,20,22,24,26,28,30},{17..., dimensions={0} | all-to-all | bytes 458752 | tf_op jit(solution)/shard_map/all_to_all | solution.py:65
  53.4 12.6 %all_to_all.26 = f32[8,56,128]{2,1,0:T(8,128)S(1)} all-to-all(f32[8,56,128]{2,1,0:T(8,128)S(1)} %broadcast_in_dim.11), channel_id=1, replica_groups={{0,2,4,6,8,10,12,14},{1,3,5,7,9,11,13,15},{16,18,20,22,24,26,28,30},{17..., dimensions={0} | all-to-all | bytes 458752 | tf_op jit(solution)/shard_map/all_to_all | solution.py:67
  66.1 0.0 copy-start.6
  66.1 0.0 collective-permute-start.1
  66.1 1.5 collective-permute-done.1
  67.5 0.0 copy-start.7
  67.5 1.0 fusion.5
  68.6 2.4 %fusion.2 = f32[256,1152]{1,0:T(8,128)S(1)} fusion(f32[448,1152]{1,0:T(8,128)S(1)} %copy-done, bf16[448,1152]{1,0:T(8,128)(2,1)S(1)} %copy-done.1, f32[448,128]{1,0:T(8,128)S(1)} %collective-permute-done.1, f32[448,128]{1,0:T(8,128)S(1)} %bitcast.19, pred[]{:T(512)S(6)} %eq.17), kind=kOutput, calls=%fused_computation.8 | convolution fusion | flops 1586823168 | bytes 4734977 | tf_op jit(solution)/shard_map/dot_general | solution.py:42
  71.0 0.0 copy-done.6
  71.0 0.0 copy-done.7
  71.0 0.1 broadcast_in_dim.12
  71.1 0.1 pad_maximum_fusion
  71.2 28.8 %all_to_all.27 = f32[16,16,1664]{2,1,0:T(8,128)S(1)} all-to-all(f32[16,16,1664]{2,1,0:T(8,128)S(1)} %pad_maximum_fusion), channel_id=1, replica_groups=mesh['row'=16,'col'=16] {'row'}, dimensions={0} | all-to-all | bytes 3407872 | tf_op jit(solution)/shard_map/all_to_all | solution.py:194
  100.0 0.6 collective-permute-start.2
  100.6 0.1 slice_reduce_fusion
  100.7 3.3 %collective-permute-done.2 = f32[32,256]{1,0:T(8,128)S(1)} collective-permute-done((f32[32,256]{1,0:T(8,128)S(1)}, f32[32,256]{1,0:T(8,128)S(1)}, u32[]{:S(2)}, u32[]{:S(2)}) %collective-permute-start.2) | collective-permute-done | bytes 32800 | tf_op jit(solution)/shard_map/ppermute | solution.py:85
  104.0 1.1 broadcast_in_dim.13
  105.1 5.1 %all-to-all-start.4 = ((f32[16,16,1152]{2,1,0:T(8,128)}), f32[16,16,1152]{2,1,0:T(8,128)S(1)}, u32[]{:S(2)}, u32[]{:S(2)}) async-start(f32[16,16,1152]{2,1,0:T(8,128)} %broadcast_in_dim.13), calls=%async_computation.4 | async-start | bytes 2359296 | tf_op jit(solution)/shard_map/all_to_all | solution.py:49
  110.2 0.5 collective-permute-start.3
  110.7 5.0 %collective-permute-done.3 = f32[64,256]{1,0:T(8,128)S(1)} collective-permute-done((f32[64,256]{1,0:T(8,128)S(1)}, f32[64,256]{1,0:T(8,128)S(1)}, u32[]{:S(2)}, u32[]{:S(2)}) %collective-permute-start.3) | collective-permute-done | bytes 65568 | tf_op jit(solution)/shard_map/ppermute | solution.py:87
  115.7 0.3 collective-permute-start.4
  116.0 1.3 collective-permute-done.4
  117.4 0.7 maximum_select_fusion.1.gram_ref
  118.1 9.8 %shard_map.67 = f32[256,256]{1,0:T(8,128)} custom-call(f32[256,256]{1,0:T(8,128)} %maximum_select_fusion.1.gram_ref), custom_call_target="tpu_custom_call" | custom-call | flops 33554432 | bytes 524288 | tf_op jit(solution)/shard_map/pallas_call | solution.py:172
  127.9 0.0 copy-start.4
  127.9 0.0 all-to-all-done.4
  127.9 0.0 copy-start.3
  127.9 1.0 copy-done.3
  128.9 2.7 %multiply_reduce_fusion = (f32[256]{0:T(256)S(1)}, f32[256,1152]{1,0:T(8,128)S(1)}) fusion(f32[256,256]{1,0:T(8,128)} %shard_map.67, f32[256,1152]{1,0:T(8,128)} %bitcast.16), kind=kOutput, calls=%fused_computation.7 | convolution fusion | flops 906559232 | bytes 2622464 | tf_op jit(solution)/shard_map/dot_general | solution.py:42
  131.6 0.2 collective-permute-start.5
  131.8 1.0 collective-permute-done.5
  132.8 0.0 collective-permute-start.6
  132.8 0.0 copy-start.2
  132.8 3.6 %collective-permute-done.6 = f32[1,256]{1,0:T(1,128)S(1)} collective-permute-done((f32[1,256]{1,0:T(1,128)S(1)}, f32[1,256]{1,0:T(1,128)S(1)}, u32[]{:S(2)}, u32[]{:S(2)}) %collective-permute-start.6) | collective-permute-done | bytes 1056 | tf_op jit(solution)/shard_map/ppermute | solution.py:94
  136.4 0.5 collective-permute-start.7
  136.9 0.0 copy-done.4
  136.9 1.8 %fusion.4 = f32[448,256]{1,0:T(8,128)S(1)} fusion(f32[256,256]{1,0:T(8,128)S(1)} %copy-done.4, f32[448,128]{1,0:T(8,128)} %copy-done.7, f32[448,128]{1,0:T(8,128)} %bitcast.20, pred[]{:T(512)S(6)} %eq.17), kind=kOutput, calls=%fused_computation.16 | convolution fusion | flops 352665600 | bytes 1179649 | tf_op jit(solution)/shard_map/dot_general | solution.py:42
  138.7 2.5 %collective-permute-done.7 = f32[1,256]{1,0:T(1,128)S(1)} collective-permute-done((f32[1,256]{1,0:T(1,128)S(1)}, f32[1,256]{1,0:T(1,128)S(1)}, u32[]{:S(2)}, u32[]{:S(2)}) %collective-permute-start.7) | collective-permute-done | bytes 1056 | tf_op jit(solution)/shard_map/ppermute | solution.py:94
  141.2 0.3 collective-permute-start.8
  141.5 0.0 copy-done.2
  141.5 2.6 %fusion.1 = f32[448,1152]{1,0:T(8,128)} fusion(f32[448,256]{1,0:T(8,128)S(1)} %fusion.4, f32[256,1152]{1,0:T(8,128)S(1)} %get-tuple-element.12, f32[448,1152]{1,0:T(8,128)S(1)} %copy-done, bf16[448,1152]{1,0:T(8,128)(2,1)S(1)} %copy-done.2), kind=kOutput, calls=%fused_computation.3 | convolution fusion | flops 794787840 | bytes 6799360 | tf_op jit(solution)/shard_map/dot_general | solution.py:42
  144.1 0.0 copy-start.5
  144.1 2.5 %collective-permute-done.8 = f32[1,256]{1,0:T(1,128)S(1)} collective-permute-done((f32[1,256]{1,0:T(1,128)S(1)}, f32[1,256]{1,0:T(1,128)S(1)}, u32[]{:S(2)}, u32[]{:S(2)}) %collective-permute-start.8) | collective-permute-done | bytes 1056 | tf_op jit(solution)/shard_map/ppermute | solution.py:94
  146.6 0.1 broadcast_multiply_fusion
  146.7 0.0 copy-done.5
  146.7 2.6 %fusion = f32[448,1152]{1,0:T(8,128)} fusion(f32[448,256]{1,0:T(8,128)S(1)} %fusion.4, f32[256,1152]{1,0:T(8,128)S(1)} %broadcast_multiply_fusion, f32[448,1152]{1,0:T(8,128)S(1)} %copy-done.5), kind=kOutput, calls=%fused_computation.1 | convolution fusion | flops 794271744 | bytes 5767168 | tf_op jit(solution)/shard_map/dot_general | solution.py:42
  149.3 0.6 constant_dynamic-slice_fusion
  (13 shorter events, 0.1 us)
Async XLA Ops:
  0.6 26.2 %copy-start = (f32[448,1152]{1,0:T(8,128)S(1)}, f32[448,1152]{1,0:T(8,128)}, u32[]{:S(2)}) copy-start(f32[448,1152]{1,0:T(8,128)} %param.4) | copy-start | bytes 6193156
  0.6 26.2 %copy-start.1 = (bf16[448,1152]{1,0:T(8,128)(2,1)S(1)}, bf16[448,1152]{1,0:T(8,128)(2,1)}, u32[]{:S(2)}) copy-start(bf16[448,1152]{1,0:T(8,128)(2,1)} %param.5) | copy-start | bytes 3096580
  2.8 24.1 %all-to-all-start = ((f32[16,16,1152]{2,1,0:T(8,128)}), f32[16,16,1152]{2,1,0:T(8,128)}, u32[]{:S(2)}, u32[]{:S(2)}) async-start(f32[16,16,1152]{2,1,0:T(8,128)} %broadcast_in_dim.10), calls=%async_computation | async-start | bytes 2359296 | tf_op jit(solution)/shard_map/all_to_all | solution.py:49
  30.8 1.8 %collective-permute-start = (f32[448,128]{1,0:T(8,128)}, f32[448,128]{1,0:T(8,128)}, u32[]{:S(2)}, u32[]{:S(2)}) collective-permute-start(f32[448,128]{1,0:T(8,128)} %constant_dynamic-slice_fusion.3), channel_id=1, source_target_pairs={{0,1},{1,0},{2,3},{3,2},{4,5},{5,4},{6,7},{7,6},{8,9},{9,8},{10,11... | collective-permute-start | bytes 688136 | tf_op jit(solution)/shard_map/ppermute | solution.py:63
  66.1 4.9 %copy-start.6 = (f32[8,56,128]{2,1,0:T(8,128)}, f32[8,56,128]{2,1,0:T(8,128)S(1)}, u32[]{:S(2)}) copy-start(f32[8,56,128]{2,1,0:T(8,128)S(1)} %all_to_all.26) | copy-start | bytes 688132
  66.1 1.5 collective-permute-start.1
  67.5 3.4 %copy-start.7 = (f32[448,128]{1,0:T(8,128)}, f32[448,128]{1,0:T(8,128)S(1)}, u32[]{:S(2)}) copy-start(f32[448,128]{1,0:T(8,128)S(1)} %collective-permute-done.1) | copy-start | bytes 688132
  100.0 4.0 %collective-permute-start.2 = (f32[32,256]{1,0:T(8,128)S(1)}, f32[32,256]{1,0:T(8,128)S(1)}, u32[]{:S(2)}, u32[]{:S(2)}) collective-permute-start(f32[32,256]{1,0:T(8,128)S(1)} %pad_maximum_fusion.2), channel_id=1, source_target_pairs={{0,2},{1,3},{2,0},{3,1},{4,6},{5,7},{6,4},{7,5},{8,10},{9,11},{10,... | collective-permute-start | bytes 98312 | tf_op jit(solution)/shard_map/ppermute | solution.py:85
  105.1 22.8 %all-to-all-start.4 = ((f32[16,16,1152]{2,1,0:T(8,128)}), f32[16,16,1152]{2,1,0:T(8,128)S(1)}, u32[]{:S(2)}, u32[]{:S(2)}) async-start(f32[16,16,1152]{2,1,0:T(8,128)} %broadcast_in_dim.13), calls=%async_computation.4 | async-start | bytes 2359296 | tf_op jit(solution)/shard_map/all_to_all | solution.py:49
  110.2 5.6 %collective-permute-start.3 = (f32[64,256]{1,0:T(8,128)S(1)}, f32[64,256]{1,0:T(8,128)S(1)}, u32[]{:S(2)}, u32[]{:S(2)}) collective-permute-start(f32[64,256]{1,0:T(8,128)S(1)} %maximum_select_fusion.6), channel_id=1, source_target_pairs={{0,14},{1,15},{2,4},{3,5},{4,2},{5,3},{6,8},{7,9},{8,6},{9,7},{10,... | collective-permute-start | bytes 196616 | tf_op jit(solution)/shard_map/ppermute | solution.py:87
  115.7 1.6 %collective-permute-start.4 = (f32[128,256]{1,0:T(8,128)S(1)}, f32[128,256]{1,0:T(8,128)S(1)}, u32[]{:S(2)}, u32[]{:S(2)}) collective-permute-start(f32[128,256]{1,0:T(8,128)S(1)} %maximum_select_fusion.2), channel_id=1, source_target_pairs={{0,1},{1,0},{2,3},{3,2},{4,5},{5,4},{6,7},{7,6},{8,9},{9,8},{10,11... | collective-permute-start | bytes 393224 | tf_op jit(solution)/shard_map/ppermute | solution.py:88
  127.9 9.0 %copy-start.4 = (f32[256,256]{1,0:T(8,128)S(1)}, f32[256,256]{1,0:T(8,128)}, u32[]{:S(2)}) copy-start(f32[256,256]{1,0:T(8,128)} %shard_map.67) | copy-start | bytes 786436
  127.9 1.0 copy-start.3
  131.6 1.2 collective-permute-start.5
  132.8 3.6 %collective-permute-start.6 = (f32[1,256]{1,0:T(1,128)S(1)}, f32[1,256]{1,0:T(1,128)S(1)}, u32[]{:S(2)}, u32[]{:S(2)}) collective-permute-start(f32[1,256]{1,0:T(1,128)S(1)} %add.81), channel_id=1, source_target_pairs={{0,2},{1,3},{2,0},{3,1},{4,6},{5,7},{6,4},{7,5},{8,10},{9,11},{10,... | collective-permute-start | bytes 3080 | tf_op jit(solution)/shard_map/ppermute | solution.py:94
  132.8 8.7 %copy-start.2 = (bf16[448,1152]{1,0:T(8,128)(2,1)S(1)}, bf16[448,1152]{1,0:T(8,128)(2,1)}, u32[]{:S(2)}) copy-start(bf16[448,1152]{1,0:T(8,128)(2,1)} %param.5) | copy-start | bytes 3096580
  136.4 4.8 %collective-permute-start.7 = (f32[1,256]{1,0:T(1,128)S(1)}, f32[1,256]{1,0:T(1,128)S(1)}, u32[]{:S(2)}, u32[]{:S(2)}) collective-permute-start(f32[1,256]{1,0:T(1,128)S(1)} %add.82), channel_id=1, source_target_pairs={{0,14},{1,15},{2,4},{3,5},{4,2},{5,3},{6,8},{7,9},{8,6},{9,7},{10,... | collective-permute-start | bytes 3080 | tf_op jit(solution)/shard_map/ppermute | solution.py:94
  141.2 5.4 %collective-permute-start.8 = (f32[1,256]{1,0:T(1,128)S(1)}, f32[1,256]{1,0:T(1,128)S(1)}, u32[]{:S(2)}, u32[]{:S(2)}) collective-permute-start(f32[1,256]{1,0:T(1,128)S(1)} %add.83), channel_id=1, source_target_pairs={{0,6},{1,7},{2,12},{3,13},{4,10},{5,11},{6,0},{7,1},{8,14},{9,15},... | collective-permute-start | bytes 3080 | tf_op jit(solution)/shard_map/ppermute | solution.py:94
  144.1 2.6 %copy-start.5 = (f32[448,1152]{1,0:T(8,128)S(1)}, f32[448,1152]{1,0:T(8,128)}, u32[]{:S(2)}) copy-start(f32[448,1152]{1,0:T(8,128)} %param.6) | copy-start | bytes 6193156

commit v4 on v3

--- a/solution.py
+++ b/solution.py
@@ -44,8 +44,8 @@
     )
 
 
-def gather_over_row(block):
-    copies = jnp.broadcast_to(block[None], (ROWS,) + block.shape)
+def gather_over_row(copies):
+    block = copies[0]
     return lax.all_to_all(copies, "row", 0, 0).reshape((ROWS * block.shape[0],) + block.shape[1:])
 
 
@@ -82,7 +82,8 @@
 def gather_bands(band, other):
     place = lax.axis_index("col")
     core, z = place % 2, place // 2
-    received, other = lax.optimization_barrier((lax.ppermute(band, "col", Z_BUTTERFLY[0]), other))
+    band, other = lax.optimization_barrier((band, other))
+    received = lax.ppermute(band, "col", Z_BUTTERFLY[0])
     mine = in_order(z % 2 == 0, band, received)
     mine = in_order(z // 2 % 2 == 0, mine, lax.ppermute(mine, "col", Z_BUTTERFLY[1]))
     return in_order(core == 0, mine, lax.ppermute(mine, "col", CORE_SWAP)), other
@@ -90,9 +91,8 @@
 
 def sum_small_over_col(value):
     value = value + lax.ppermute(value, "col", CORE_SWAP)
-    for pairs in Z_BUTTERFLY:
-        value = value + lax.ppermute(value, "col", pairs)
-    return value
+    copies = jnp.broadcast_to(value[None], (DEPTH,) + value.shape)
+    return jnp.sum(lax.all_to_all(copies, "col", 0, 0, axis_index_groups=Z_GROUPS), axis=0)
 
 
 BAND = 32
@@ -104,7 +104,10 @@
     n = out_ref.shape[0]
     groups, tiles = BAND // SUB, n // LANES
     row_of = lax.broadcasted_iota(jnp.int32, (SUB, LANES), 0)
-    work[...] = gram_ref[...]
+    half = n // 2
+    work[:half, :] = gram_ref[:, :n]
+    work[half:, :half] = jnp.zeros((n - half, half), jnp.float32)
+    work[half:, half:] = gram_ref[:, n:]
     for start in range(0, n, BAND):
         columns = [
             [
@@ -151,11 +154,17 @@
                 work[start + SUB * g : start + SUB * (g + 1), LANES * t : LANES * (t + 1)] = rows[g][t]
         below = n - start - BAND
         if below:
+            value = work[start : start + BAND, :]
+            first = value.astype(jnp.bfloat16)
+            rest = value - first.astype(jnp.float32)
+            second = rest.astype(jnp.bfloat16)
+            third = (rest - second.astype(jnp.float32)).astype(jnp.bfloat16)
+            left = jnp.concatenate([first, first, second, second, first, third], 0)
+            right = jnp.concatenate([first, second, first, second, third, first], 0)
             update = lax.dot_general(
-                work[start : start + BAND, start + BAND :],
-                work[start : start + BAND, :],
+                left[:, start + BAND :],
+                right,
                 (((0,), (0,)), ((), ())),
-                precision=HIGHEST,
                 preferred_element_type=jnp.float32,
             )
             place = lax.broadcasted_iota(jnp.int32, (below, n), 1) - start
@@ -166,42 +175,111 @@
     out_ref[...] = jnp.where(row >= column, work[...], 0.0)
 
 
-def inverse_factor(gram_and_more):
-    n = gram_and_more.shape[0]
-    block = pl.BlockSpec((n, n), lambda i: (0, 0))
+def inverse_factor(packed):
+    n = 2 * packed.shape[0]
     return pl.pallas_call(
         inverse_factor_kernel,
-        grid=(1,),
         out_shape=jax.ShapeDtypeStruct((n, n), jnp.float32),
-        in_specs=[block],
-        out_specs=block,
+        in_specs=[pl.BlockSpec(memory_space=pltpu.VMEM)],
+        out_specs=pl.BlockSpec(memory_space=pltpu.VMEM),
         scratch_shapes=[pltpu.VMEM((n, n), jnp.float32)],
+        compiler_params=pltpu.CompilerParams(vmem_limit_bytes=6 * 2**20),
         cost_estimate=pl.CostEstimate(flops=2 * n**3, bytes_accessed=8 * n * n, transcendentals=n),
-    )(gram_and_more)
+    )(packed)
+
+
+def right_product_kernel(inverse_ref, cross_ref, out_ref, squares_ref, total):
+    step = pl.program_id(0)
+    value = product(inverse_ref[...], cross_ref[...], ((1,), (0,)))
+    out_ref[...] = value
+    squared = value * value
+    tiles = [squared[:, LANES * t : LANES * (t + 1)] for t in range(value.shape[1] // LANES)]
+
+    @pl.when(step == 0)
+    def _():
+        total[...] = sum(tiles)
+
+    @pl.when(step > 0)
+    def _():
+        total[...] += sum(tiles)
+
+    @pl.when(step == pl.num_programs(0) - 1)
+    def _():
+        squares_ref[...] = jnp.sum(total[...].T, axis=0, keepdims=True)
+
+
+def right_product_and_squares(inverse, cross):
+    rank, columns = cross.shape
+    block = 3 * LANES
+    whole = pl.BlockSpec((rank, rank), lambda i: (0, 0))
+    strip = pl.BlockSpec((rank, block), lambda i: (0, i))
+    return pl.pallas_call(
+        right_product_kernel,
+        grid=(columns // block,),
+        out_shape=(
+            jax.ShapeDtypeStruct(cross.shape, jnp.float32),
+            jax.ShapeDtypeStruct((1, rank), jnp.float32),
+        ),
+        in_specs=[whole, strip],
+        out_specs=(strip, pl.BlockSpec((1, rank), lambda i: (0, 0))),
+        scratch_shapes=[pltpu.VMEM((rank, LANES), jnp.float32)],
+        compiler_params=pltpu.CompilerParams(vmem_limit_bytes=8 * 2**20),
+        cost_estimate=pl.CostEstimate(
+            flops=12 * rank * rank * columns, bytes_accessed=8 * cross.size, transcendentals=0
+        ),
+    )(inverse, cross)
+
+
+def repeat_kernel(block_ref, out_ref, semaphores):
+    copies = [
+        pltpu.make_async_copy(block_ref, out_ref.at[i], semaphores.at[i])
+        for i in range(out_ref.shape[0])
+    ]
+    for copy in copies:
+        copy.start()
+    for copy in copies:
+        copy.wait()
+
+
+def repeat(block, times):
+    return pl.pallas_call(
+        repeat_kernel,
+        out_shape=jax.ShapeDtypeStruct((times,) + block.shape, block.dtype),
+        in_specs=[pl.BlockSpec(memory_space=pl.ANY)],
+        out_specs=pl.BlockSpec(memory_space=pl.ANY),
+        scratch_shapes=[pltpu.SemaphoreType.DMA((times,))],
+        compiler_params=pltpu.CompilerParams(vmem_limit_bytes=2**20),
+        cost_estimate=pl.CostEstimate(
+            flops=0, bytes_accessed=8 * times * block.size, transcendentals=0
+        ),
+    )(block)
 
 
 def per_device(momentum, gradient, weight, right_factor):
     summed = momentum + gradient.astype(jnp.float32)
-    right_all = gather_over_row(right_factor)
+    right_all = gather_over_row(repeat(right_factor, ROWS))
     projected = sum_over_col(product(summed, right_all, ((1,), (1,))))
     local_cross = product(projected, summed, ((0,), (0,)))
+    half = RANK // 2
     local_gram = product(projected, projected, ((0,), (0,)))
-    rows, band = RANK // ROWS, RANK // 8
-    at = band_index() * band
-    band_parts = [lax.dynamic_slice_in_dim(local_gram, at + i, rows, 0) for i in range(0, band, rows)]
-    bands = jnp.broadcast_to(jnp.concatenate(band_parts, 1)[None], (ROWS, rows, RANK * band // rows))
+    rows, columns = RANK // ROWS, summed.shape[1]
+    at = band_index() * rows
+    band = jnp.concatenate(
+        [
+            lax.dynamic_slice_in_dim(local_gram, at, rows, 0),
+            lax.dynamic_slice_in_dim(local_gram, at + half, rows, 0)[:, half:],
+        ],
+        1,
+    )
+    bands = jnp.broadcast_to(band[None], (ROWS,) + band.shape)
     parts = jnp.concatenate([local_cross.reshape(ROWS, rows, -1), bands], axis=2)
     taken = lax.all_to_all(parts, "row", 0, 0)
-    columns = summed.shape[1]
     gram_band = jnp.sum(taken[:, :, columns:], axis=0)
-    gram_band = jnp.concatenate(
-        [gram_band[:, i * RANK : (i + 1) * RANK] for i in range(band // rows)], 0
-    )
-    gram_matrix, cross_part = gather_bands(gram_band, jnp.sum(taken[:, :, :columns], axis=0))
-    cross = gather_over_row(cross_part)
-    lower_inverse = inverse_factor(gram_matrix)
-    right_product = product(lower_inverse, cross, ((1,), (0,)))
-    squares = sum_small_over_col(jnp.sum(right_product * right_product, axis=1)[None])[0]
+    packed, cross_part = gather_bands(gram_band, jnp.sum(taken[:, :, :columns], axis=0))
+    cross = gather_over_row(jnp.broadcast_to(cross_part[None], (ROWS,) + cross_part.shape))
+    lower_inverse = inverse_factor(packed)
+    right_product, squares = right_product_and_squares(lower_inverse, cross)
+    squares = sum_small_over_col(squares)[0]
     ortho = product(projected, lower_inverse, ((1,), (1,)))
     momentum_delta = product(ortho, right_product, ((1,), (0,)), lax.Precision.HIGH)
     new_momentum = summed - (1.0 - momentum_keep) * momentum_delta

time: 150 us -> 143 us (0.953)
  waiting for transfers between devices: 39.1 us -> 33.3 us
  starting transfers between devices: 15 us -> 18.3 us
  matrix products: 16.3 us -> 14 us
  blocking collectives: 61.1 us -> 59 us
    ppermute x4 -> x1, waiting for transfers between devices: 11.8 us -> 3.31 us  [gather_bands(): received = lax.ppermute(band, 'col', Z_BUTTERFLY[0])]
    all_to_all x0 -> x1, waiting for transfers between devices: none -> 3.55 us  [sum_small_over_col(): lax.all_to_all(copies, 'col', 0, 0, axis_index_groups=Z_GROUPS)]
    all_to_all x0 -> x1, starting transfers between devices: none -> 3.33 us  [sum_small_over_col(): lax.all_to_all(copies, 'col', 0, 0, axis_index_groups=Z_GROUPS)]
    dot_general x7 -> x6, matrix products: 16.3 us -> 14 us  [product(): lax.dot_general(a, b, (contract, ((), ())), precision=precision, preferre...]
    all_to_all x1, blocking collectives: 28.8 us -> 26.7 us  [per_device(): taken = lax.all_to_all(parts, 'row', 0, 0)]
    broadcast_in_dim x3, local copies, waits for them, and re-layouts: 3.26 us -> 1.72 us  [the longest x1 1.09 us: per_device(): jnp.broadcast_to(cross_part[None], (ROWS,) + cross_part.shape)]
    pallas_call x1 -> x3, Pallas kernels: 9.82 us -> 10.4 us  [the longest x1 7.03 us: inverse_factor(): pl.pallas_call(inverse_factor_kernel, out_shape=jax.ShapeDtypeStruct((n,...]
  transfers between devices with their start and end apart: 11 -> 9, of which waited for: 10 -> 8; matrix products, arithmetic and copies ran while one was open for 3% -> 3% of each run, Pallas kernels for 7% -> 5%
where the time goes in v4:
time: 143 us
  blocking collectives  59 us (41%)
  waiting for transfers between devices  33.3 us (23%)
  starting transfers between devices  18.3 us (13%)
  matrix products  14 us (10%)
  Pallas kernels  10.4 us (7%)
  local copies, waits for them, and re-layouts  5.42 us (4%)
  other arithmetic  1.46 us (1%)
    all_to_all x1, blocking collectives, per_device(): taken = lax.all_to_all(parts, 'row', 0, 0)  26.7 us
    all_to_all x1, blocking collectives, sum_over_col(): lax.all_to_all(parts, 'col', 0, 0, axis_index_groups=Z_GROUPS)  19.7 us
    all_to_all x2, waiting for transfers between devices, gather_over_row(): lax.all_to_all(copies, 'row', 0, 0)  16.6 us
    dot_general x6, matrix products, product(): lax.dot_general(a, b, (contract, ((), ())), precision=precision, preferre...  14 us
    all_to_all x2, starting transfers between devices, gather_over_row(): lax.all_to_all(copies, 'row', 0, 0)  13.5 us
    all_to_all x1, blocking collectives, sum_over_col(): lax.all_to_all(copies, 'col', 0, 0, axis_index_groups=Z_GROUPS)  12.6 us
    pallas_call x1, Pallas kernels, inverse_factor(): pl.pallas_call(inverse_factor_kernel, out_shape=jax.ShapeDtypeStruct((n,...  7.03 us
    ppermute x1, waiting for transfers between devices, gather_bands(): lax.ppermute(mine, 'col', Z_BUTTERFLY[1])  4.84 us
  transfers between devices with their start and end apart: 9, of which 8 were waited for; matrix products, arithmetic and copies ran while one was open for 3% of the time, Pallas kernels for 5%

profile of v4, /device:TPU:2, one launch (start us, length us, event | category | flops | bytes accessed | tf_op | source)
XLA Modules:
  0.0 142.7 jit_solution(9275621001792086920)
XLA Ops:
  0.6 0.0 copy-start
  0.6 0.9 copy-done
  1.5 0.0 copy-start.1
  1.5 0.0 copy-start.2
  1.5 1.1 shard_map.67
  2.7 7.6 %all-to-all-start = ((f32[16,16,1152]{2,1,0:T(8,128)}), f32[16,16,1152]{2,1,0:T(8,128)}, u32[]{:S(2)}, u32[]{:S(2)}) async-start(f32[16,16,1152]{2,1,0:T(8,128)} %shard_map.67), calls=%async_computation | async-start | bytes 2359296 | tf_op jit(solution)/shard_map/all_to_all | solution.py:49
  10.3 16.6 %all-to-all-done = f32[16,16,1152]{2,1,0:T(8,128)} async-done(((f32[16,16,1152]{2,1,0:T(8,128)}), f32[16,16,1152]{2,1,0:T(8,128)}, u32[]{:S(2)}, u32[]{:S(2)}) %all-to-all-start) | async-done | bytes 1179680 | tf_op jit(solution)/shard_map/all_to_all | solution.py:49
  26.9 0.0 copy-done.1
  26.9 0.0 copy-done.2
  26.9 3.3 %fusion.3 = f32[448,256]{1,0:T(8,128)S(1)} fusion(f32[256,1152]{1,0:T(8,128)} %bitcast, f32[448,1152]{1,0:T(8,128)S(1)} %copy-done.1, bf16[448,1152]{1,0:T(8,128)(2,1)S(1)} %copy-done.2), kind=kOutput, calls=%fused_computation.8 | convolution fusion | flops 1586479104 | bytes 4734976 | tf_op jit(solution)/shard_map/dot_general | solution.py:42
  30.2 0.7 constant_dynamic-slice_fusion.2
  30.9 0.0 collective-permute-start
  30.9 1.8 %collective-permute-done = f32[448,128]{1,0:T(8,128)} collective-permute-done((f32[448,128]{1,0:T(8,128)}, f32[448,128]{1,0:T(8,128)}, u32[]{:S(2)}, u32[]{:S(2)}) %collective-permute-start) | collective-permute-done | bytes 229408 | tf_op jit(solution)/shard_map/ppermute | solution.py:63
  32.7 1.0 dynamic-slice_add_fusion
  33.7 19.7 %all_to_all.30 = f32[8,56,128]{2,1,0:T(8,128)S(1)} all-to-all(f32[8,56,128]{2,1,0:T(8,128)S(1)} %bitcast.18), channel_id=1, replica_groups={{0,2,4,6,8,10,12,14},{1,3,5,7,9,11,13,15},{16,18,20,22,24,26,28,30},{17..., dimensions={0} | all-to-all | bytes 458752 | tf_op jit(solution)/shard_map/all_to_all | solution.py:65
  53.5 12.6 %all_to_all.31 = f32[8,56,128]{2,1,0:T(8,128)S(1)} all-to-all(f32[8,56,128]{2,1,0:T(8,128)S(1)} %broadcast_in_dim.10), channel_id=1, replica_groups={{0,2,4,6,8,10,12,14},{1,3,5,7,9,11,13,15},{16,18,20,22,24,26,28,30},{17..., dimensions={0} | all-to-all | bytes 458752 | tf_op jit(solution)/shard_map/all_to_all | solution.py:67
  66.1 0.0 collective-permute-start.1
  66.1 1.5 %collective-permute-done.1 = f32[448,128]{1,0:T(8,128)S(1)} collective-permute-done((f32[448,128]{1,0:T(8,128)S(1)}, f32[448,128]{1,0:T(8,128)S(1)}, u32[]{:S(2)}, u32[]{:S(2)}) %collective-permute-start.1) | collective-permute-done | bytes 229408 | tf_op jit(solution)/shard_map/ppermute | solution.py:68
  67.6 1.0 fusion.5
  68.6 2.4 %fusion.2 = f32[256,1152]{1,0:T(8,128)S(1)} fusion(f32[448,1152]{1,0:T(8,128)S(1)} %copy-done.1, bf16[448,1152]{1,0:T(8,128)(2,1)S(1)} %copy-done.2, f32[448,128]{1,0:T(8,128)S(1)} %collective-permute-done.1, f32[448,128]{1,0:T(8,128)S(1)} %bitcast.16, pred[]{:T(512)S(6)} %eq.17), kind=kOutput, calls=%fused_computation.7 | convolution fusion | flops 1586823168 | bytes 4734977 | tf_op jit(solution)/shard_map/dot_general | solution.py:42
  71.1 0.2 pad_maximum_fusion
  71.2 26.7 %all_to_all.32 = f32[16,16,1536]{2,1,0:T(8,128)S(1)} all-to-all(f32[16,16,1536]{2,1,0:T(8,128)S(1)} %pad_maximum_fusion), channel_id=1, replica_groups=mesh['row'=16,'col'=16] {'row'}, dimensions={0} | all-to-all | bytes 3145728 | tf_op jit(solution)/shard_map/all_to_all | solution.py:276
  97.9 0.1 slice_reduce_fusion
  98.0 1.1 broadcast_in_dim.12
  99.1 5.9 %all-to-all-start.4 = ((f32[16,16,1152]{2,1,0:T(8,128)}), f32[16,16,1152]{2,1,0:T(8,128)S(1)}, u32[]{:S(2)}, u32[]{:S(2)}) async-start(f32[16,16,1152]{2,1,0:T(8,128)} %broadcast_in_dim.12), calls=%async_computation.4 | async-start | bytes 2359296 | tf_op jit(solution)/shard_map/all_to_all | solution.py:49
  105.0 0.5 collective-permute-start.2
  105.5 3.3 %collective-permute-done.2 = f32[16,384]{1,0:T(8,128)S(1)} collective-permute-done((f32[16,384]{1,0:T(8,128)S(1)}, f32[16,384]{1,0:T(8,128)S(1)}, u32[]{:S(2)}, u32[]{:S(2)}) %collective-permute-start.2) | collective-permute-done | bytes 24608 | tf_op jit(solution)/shard_map/ppermute | solution.py:86
  108.8 0.5 collective-permute-start.3
  109.3 4.8 %collective-permute-done.3 = f32[32,384]{1,0:T(8,128)S(1)} collective-permute-done((f32[32,384]{1,0:T(8,128)S(1)}, f32[32,384]{1,0:T(8,128)S(1)}, u32[]{:S(2)}, u32[]{:S(2)}) %collective-permute-start.3) | collective-permute-done | bytes 49184 | tf_op jit(solution)/shard_map/ppermute | solution.py:88
  114.1 0.3 collective-permute-start.4
  114.4 1.3 collective-permute-done.4
  115.7 7.0 %shard_map.68.inverse_ref = f32[256,256]{1,0:T(8,128)S(1)} custom-call(f32[128,384]{1,0:T(8,128)S(1)} %maximum_select_fusion.1.gram_ref), custom_call_target="tpu_custom_call" | custom-call | flops 33554432 | bytes 524288 | tf_op jit(solution)/shard_map/pallas_call | solution.py:180
  122.8 0.0 all-to-all-done.4
  122.8 2.2 %shard_map.69 = (f32[256,1152]{1,0:T(8,128)S(1)}, f32[1,256]{1,0:T(1,128)S(1)}) custom-call(f32[256,256]{1,0:T(8,128)S(1)} %shard_map.68.inverse_ref, f32[256,1152]{1,0:T(8,128)S(1)} %bitcast.12), custom_call_target="tpu_custom_call" | custom-call | flops 905969664 | bytes 2359296 | tf_op jit(solution)/shard_map/pallas_call | solution.py:216
  125.0 0.0 copy-start.3
  125.0 0.2 collective-permute-start.5
  125.2 0.6 fusion.4
  125.8 0.4 collective-permute-done.5
  126.2 0.6 broadcast_in_dim.14
  126.8 3.3 %all-to-all-start.5 = ((f32[8,1,256]{2,1,0:T(1,128)}), f32[8,1,256]{2,1,0:T(1,128)S(1)}, u32[]{:S(2)}, u32[]{:S(2)}) async-start(f32[8,1,256]{2,1,0:T(1,128)} %broadcast_in_dim.14), calls=%async_computation.5 | async-start | bytes 16384 | tf_op jit(solution)/shard_map/all_to_all | solution.py:95
  130.2 0.0 copy-done.3
  130.2 4.1 %fusion.1 = f32[448,1152]{1,0:T(8,128)} fusion(f32[448,256]{1,0:T(8,128)S(1)} %fusion.4, f32[256,1152]{1,0:T(8,128)S(1)} %get-tuple-element.9, f32[448,1152]{1,0:T(8,128)} %param.4, bf16[448,1152]{1,0:T(8,128)(2,1)S(1)} %copy-done.3), kind=kOutput, calls=%fused_computation.3 | convolution fusion | flops 794787840 | bytes 6799360 | tf_op jit(solution)/shard_map/dot_general | solution.py:42
  134.3 3.6 %all-to-all-done.5 = f32[8,1,256]{2,1,0:T(1,128)S(1)} async-done(((f32[8,1,256]{2,1,0:T(1,128)}), f32[8,1,256]{2,1,0:T(1,128)S(1)}, u32[]{:S(2)}, u32[]{:S(2)}) %all-to-all-start.5) | async-done | bytes 8224 | tf_op jit(solution)/shard_map/all_to_all | solution.py:95
  137.9 0.0 copy-start.4
  137.9 0.1 broadcast_multiply_fusion
  138.0 1.4 copy-done.4
  139.4 2.6 %fusion = f32[448,1152]{1,0:T(8,128)} fusion(f32[448,256]{1,0:T(8,128)S(1)} %fusion.4, f32[256,1152]{1,0:T(8,128)S(1)} %broadcast_multiply_fusion, f32[448,1152]{1,0:T(8,128)S(1)} %copy-done.4), kind=kOutput, calls=%fused_computation.1 | convolution fusion | flops 794271744 | bytes 5767168 | tf_op jit(solution)/shard_map/dot_general | solution.py:42
  142.1 0.6 constant_dynamic-slice_fusion
  (13 shorter events, 0.2 us)
Async XLA Ops:
  0.6 0.9 copy-start
  1.5 25.4 %copy-start.1 = (f32[448,1152]{1,0:T(8,128)S(1)}, f32[448,1152]{1,0:T(8,128)}, u32[]{:S(2)}) copy-start(f32[448,1152]{1,0:T(8,128)} %param.4) | copy-start | bytes 6193156
  1.5 25.4 %copy-start.2 = (bf16[448,1152]{1,0:T(8,128)(2,1)S(1)}, bf16[448,1152]{1,0:T(8,128)(2,1)}, u32[]{:S(2)}) copy-start(bf16[448,1152]{1,0:T(8,128)(2,1)} %param.5) | copy-start | bytes 3096580
  2.7 24.2 %all-to-all-start = ((f32[16,16,1152]{2,1,0:T(8,128)}), f32[16,16,1152]{2,1,0:T(8,128)}, u32[]{:S(2)}, u32[]{:S(2)}) async-start(f32[16,16,1152]{2,1,0:T(8,128)} %shard_map.67), calls=%async_computation | async-start | bytes 2359296 | tf_op jit(solution)/shard_map/all_to_all | solution.py:49
  30.9 1.8 %collective-permute-start = (f32[448,128]{1,0:T(8,128)}, f32[448,128]{1,0:T(8,128)}, u32[]{:S(2)}, u32[]{:S(2)}) collective-permute-start(f32[448,128]{1,0:T(8,128)} %constant_dynamic-slice_fusion.2), channel_id=1, source_target_pairs={{0,1},{1,0},{2,3},{3,2},{4,5},{5,4},{6,7},{7,6},{8,9},{9,8},{10,11... | collective-permute-start | bytes 688136 | tf_op jit(solution)/shard_map/ppermute | solution.py:63
  66.1 1.5 %collective-permute-start.1 = (f32[448,128]{1,0:T(8,128)S(1)}, f32[448,128]{1,0:T(8,128)S(1)}, u32[]{:S(2)}, u32[]{:S(2)}) collective-permute-start(f32[448,128]{1,0:T(8,128)S(1)} %bitcast.14), channel_id=1, source_target_pairs={{0,1},{1,0},{2,3},{3,2},{4,5},{5,4},{6,7},{7,6},{8,9},{9,8},{10,11... | collective-permute-start | bytes 688136 | tf_op jit(solution)/shard_map/ppermute | solution.py:68
  99.1 23.7 %all-to-all-start.4 = ((f32[16,16,1152]{2,1,0:T(8,128)}), f32[16,16,1152]{2,1,0:T(8,128)S(1)}, u32[]{:S(2)}, u32[]{:S(2)}) async-start(f32[16,16,1152]{2,1,0:T(8,128)} %broadcast_in_dim.12), calls=%async_computation.4 | async-start | bytes 2359296 | tf_op jit(solution)/shard_map/all_to_all | solution.py:49
  105.0 3.8 %collective-permute-start.2 = (f32[16,384]{1,0:T(8,128)S(1)}, f32[16,384]{1,0:T(8,128)S(1)}, u32[]{:S(2)}, u32[]{:S(2)}) collective-permute-start(f32[16,384]{1,0:T(8,128)S(1)} %slice_reduce_fusion.1), channel_id=1, source_target_pairs={{0,2},{1,3},{2,0},{3,1},{4,6},{5,7},{6,4},{7,5},{8,10},{9,11},{10,... | collective-permute-start | bytes 73736 | tf_op jit(solution)/shard_map/ppermute | solution.py:86
  108.8 5.3 %collective-permute-start.3 = (f32[32,384]{1,0:T(8,128)S(1)}, f32[32,384]{1,0:T(8,128)S(1)}, u32[]{:S(2)}, u32[]{:S(2)}) collective-permute-start(f32[32,384]{1,0:T(8,128)S(1)} %maximum_select_fusion.6), channel_id=1, source_target_pairs={{0,14},{1,15},{2,4},{3,5},{4,2},{5,3},{6,8},{7,9},{8,6},{9,7},{10,... | collective-permute-start | bytes 147464 | tf_op jit(solution)/shard_map/ppermute | solution.py:88
  114.1 1.6 %collective-permute-start.4 = (f32[64,384]{1,0:T(8,128)S(1)}, f32[64,384]{1,0:T(8,128)S(1)}, u32[]{:S(2)}, u32[]{:S(2)}) collective-permute-start(f32[64,384]{1,0:T(8,128)S(1)} %maximum_select_fusion.2), channel_id=1, source_target_pairs={{0,1},{1,0},{2,3},{3,2},{4,5},{5,4},{6,7},{7,6},{8,9},{9,8},{10,11... | collective-permute-start | bytes 294920 | tf_op jit(solution)/shard_map/ppermute | solution.py:89
  125.0 5.2 %copy-start.3 = (bf16[448,1152]{1,0:T(8,128)(2,1)S(1)}, bf16[448,1152]{1,0:T(8,128)(2,1)}, u32[]{:S(2)}) copy-start(bf16[448,1152]{1,0:T(8,128)(2,1)} %param.5) | copy-start | bytes 3096580
  125.0 1.2 collective-permute-start.5
  126.8 11.0 %all-to-all-start.5 = ((f32[8,1,256]{2,1,0:T(1,128)}), f32[8,1,256]{2,1,0:T(1,128)S(1)}, u32[]{:S(2)}, u32[]{:S(2)}) async-start(f32[8,1,256]{2,1,0:T(1,128)} %broadcast_in_dim.14), calls=%async_computation.5 | async-start | bytes 16384 | tf_op jit(solution)/shard_map/all_to_all | solution.py:95
  137.9 1.6 %copy-start.4 = (f32[448,1152]{1,0:T(8,128)S(1)}, f32[448,1152]{1,0:T(8,128)}, u32[]{:S(2)}) copy-start(f32[448,1152]{1,0:T(8,128)} %param.6) | copy-start | bytes 6193156

commit v5 on v4

--- a/solution.py
+++ b/solution.py
@@ -230,29 +230,51 @@
     )(inverse, cross)
 
 
-def repeat_kernel(block_ref, out_ref, semaphores):
-    copies = [
-        pltpu.make_async_copy(block_ref, out_ref.at[i], semaphores.at[i])
-        for i in range(out_ref.shape[0])
-    ]
-    for copy in copies:
-        copy.start()
-    for copy in copies:
-        copy.wait()
+def repeat_kernel(block_ref, out_ref):
+    value = block_ref[...]
+    for i in range(out_ref.shape[0]):
+        out_ref[i] = value
 
 
 def repeat(block, times):
     return pl.pallas_call(
         repeat_kernel,
         out_shape=jax.ShapeDtypeStruct((times,) + block.shape, block.dtype),
-        in_specs=[pl.BlockSpec(memory_space=pl.ANY)],
-        out_specs=pl.BlockSpec(memory_space=pl.ANY),
-        scratch_shapes=[pltpu.SemaphoreType.DMA((times,))],
-        compiler_params=pltpu.CompilerParams(vmem_limit_bytes=2**20),
+        in_specs=[pl.BlockSpec(memory_space=pltpu.VMEM)],
+        out_specs=pl.BlockSpec(memory_space=pltpu.VMEM),
+        compiler_params=pltpu.CompilerParams(vmem_limit_bytes=4 * 2**20),
         cost_estimate=pl.CostEstimate(
-            flops=0, bytes_accessed=8 * times * block.size, transcendentals=0
+            flops=0, bytes_accessed=4 * times * block.size, transcendentals=0
         ),
     )(block)
+
+
+def sum_and_repeat_kernel(parts_ref, out_ref, rest_ref):
+    times, _, columns = out_ref.shape
+    total = parts_ref[0]
+    for i in range(1, times):
+        total = total + parts_ref[i]
+    rest_ref[...] = total[:, columns:]
+    for i in range(times):
+        out_ref[i] = total[:, :columns]
+
+
+def sum_and_repeat(parts, columns):
+    times, rows, width = parts.shape
+    vmem = pl.BlockSpec(memory_space=pltpu.VMEM)
+    return pl.pallas_call(
+        sum_and_repeat_kernel,
+        out_shape=(
+            jax.ShapeDtypeStruct((times, rows, columns), parts.dtype),
+            jax.ShapeDtypeStruct((rows, width - columns), parts.dtype),
+        ),
+        in_specs=[vmem],
+        out_specs=(vmem, vmem),
+        compiler_params=pltpu.CompilerParams(vmem_limit_bytes=6 * 2**20),
+        cost_estimate=pl.CostEstimate(
+            flops=parts.size, bytes_accessed=8 * parts.size, transcendentals=0
+        ),
+    )(parts)
 
 
 def per_device(momentum, gradient, weight, right_factor):
@@ -274,9 +296,9 @@
     bands = jnp.broadcast_to(band[None], (ROWS,) + band.shape)
     parts = jnp.concatenate([local_cross.reshape(ROWS, rows, -1), bands], axis=2)
     taken = lax.all_to_all(parts, "row", 0, 0)
-    gram_band = jnp.sum(taken[:, :, columns:], axis=0)
-    packed, cross_part = gather_bands(gram_band, jnp.sum(taken[:, :, :columns], axis=0))
-    cross = gather_over_row(jnp.broadcast_to(cross_part[None], (ROWS,) + cross_part.shape))
+    cross_copies, gram_band = sum_and_repeat(taken, columns)
+    packed, cross_copies = gather_bands(gram_band, cross_copies)
+    cross = gather_over_row(cross_copies)
     lower_inverse = inverse_factor(packed)
     right_product, squares = right_product_and_squares(lower_inverse, cross)
     squares = sum_small_over_col(squares)[0]
@@ -285,12 +307,12 @@
     new_momentum = summed - (1.0 - momentum_keep) * momentum_delta
     inverse = lax.rsqrt(squares / NDIM + epsilon)
     factor_all = right_product * inverse[:, None]
+    new_factor = lax.dynamic_slice_in_dim(
+        factor_all, lax.axis_index("row") * right_factor.shape[0], right_factor.shape[0], 0
+    )
+    factor_all, new_factor = lax.optimization_barrier((factor_all, new_factor))
     weight_delta = product(ortho, factor_all, ((1,), (0,)), lax.Precision.HIGH)
     step_scale = learn_rate * math.sqrt(MDIM / RANK)
-    band_rows = right_factor.shape[0]
-    new_factor = lax.dynamic_slice_in_dim(
-        factor_all, lax.axis_index("row") * band_rows, band_rows, 0
-    )
     new_weight = (1.0 - learn_rate * weight_decay) * weight - step_scale * weight_delta
     return (new_momentum, new_weight, new_factor)
 

time: 143 us -> 143 us (level)
  local copies, waits for them, and re-layouts: 5.42 us -> 3.71 us
where the time goes in v5:
time: 143 us; the launch traced here: 142 us
  blocking collectives  59 us (41%)
  waiting for transfers between devices  33.1 us (23%)
  starting transfers between devices  18.3 us (13%)
  matrix products  14.2 us (10%)
  Pallas kernels  11.4 us (8%)
  local copies, waits for them, and re-layouts  3.71 us (3%)
    all_to_all x1, blocking collectives, per_device(): taken = lax.all_to_all(parts, 'row', 0, 0)  26.7 us
    all_to_all x1, blocking collectives, sum_over_col(): lax.all_to_all(parts, 'col', 0, 0, axis_index_groups=Z_GROUPS)  19.7 us
    all_to_all x2, waiting for transfers between devices, gather_over_row(): lax.all_to_all(copies, 'row', 0, 0)  16.6 us
    dot_general x6, matrix products, product(): lax.dot_general(a, b, (contract, ((), ())), precision=precision, preferre...  14.2 us
    all_to_all x2, starting transfers between devices, gather_over_row(): lax.all_to_all(copies, 'row', 0, 0)  13.5 us
    all_to_all x1, blocking collectives, sum_over_col(): lax.all_to_all(copies, 'col', 0, 0, axis_index_groups=Z_GROUPS)  12.6 us
    pallas_call x1, Pallas kernels, inverse_factor(): pl.pallas_call(inverse_factor_kernel, out_shape=jax.ShapeDtypeStruct((n,...  7.03 us
    ppermute x1, waiting for transfers between devices, gather_bands(): lax.ppermute(mine, 'col', Z_BUTTERFLY[1])  4.84 us
  transfers between devices with their start and end apart: 9, of which 8 were waited for; matrix products, arithmetic and copies ran while one was open for 3% of the time, Pallas kernels for 5%

profile of v5, /device:TPU:2, one launch (start us, length us, event | category | flops | bytes accessed | tf_op | source)
XLA Modules:
  0.0 142.0 jit_solution(7671641870646208718)
XLA Ops:
  0.6 0.0 copy-start
  0.6 0.9 copy-done
  1.5 0.0 copy-start.1
  1.5 0.0 copy-start.2
  1.5 1.1 shard_map.67
  2.6 7.6 %all-to-all-start = ((f32[16,16,1152]{2,1,0:T(8,128)}), f32[16,16,1152]{2,1,0:T(8,128)}, u32[]{:S(2)}, u32[]{:S(2)}) async-start(f32[16,16,1152]{2,1,0:T(8,128)} %shard_map.67), calls=%async_computation | async-start | bytes 2359296 | tf_op jit(solution)/shard_map/all_to_all | solution.py:49
  10.2 16.6 %all-to-all-done = f32[16,16,1152]{2,1,0:T(8,128)} async-done(((f32[16,16,1152]{2,1,0:T(8,128)}), f32[16,16,1152]{2,1,0:T(8,128)}, u32[]{:S(2)}, u32[]{:S(2)}) %all-to-all-start) | async-done | bytes 1179680 | tf_op jit(solution)/shard_map/all_to_all | solution.py:49
  26.8 0.0 copy-done.1
  26.8 0.0 copy-done.2
  26.8 3.3 %fusion.3 = f32[448,256]{1,0:T(8,128)S(1)} fusion(f32[256,1152]{1,0:T(8,128)} %bitcast, f32[448,1152]{1,0:T(8,128)S(1)} %copy-done.1, bf16[448,1152]{1,0:T(8,128)(2,1)S(1)} %copy-done.2), kind=kOutput, calls=%fused_computation.7 | convolution fusion | flops 1586479104 | bytes 4734976 | tf_op jit(solution)/shard_map/dot_general | solution.py:42
  30.1 0.7 constant_dynamic-slice_fusion.2
  30.8 0.0 collective-permute-start
  30.8 1.8 %collective-permute-done = f32[448,128]{1,0:T(8,128)} collective-permute-done((f32[448,128]{1,0:T(8,128)}, f32[448,128]{1,0:T(8,128)}, u32[]{:S(2)}, u32[]{:S(2)}) %collective-permute-start) | collective-permute-done | bytes 229408 | tf_op jit(solution)/shard_map/ppermute | solution.py:63
  32.6 1.0 dynamic-slice_add_fusion
  33.6 19.7 %all_to_all.30 = f32[8,56,128]{2,1,0:T(8,128)S(1)} all-to-all(f32[8,56,128]{2,1,0:T(8,128)S(1)} %bitcast.18), channel_id=1, replica_groups={{0,2,4,6,8,10,12,14},{1,3,5,7,9,11,13,15},{16,18,20,22,24,26,28,30},{17..., dimensions={0} | all-to-all | bytes 458752 | tf_op jit(solution)/shard_map/all_to_all | solution.py:65
  53.4 12.6 %all_to_all.31 = f32[8,56,128]{2,1,0:T(8,128)S(1)} all-to-all(f32[8,56,128]{2,1,0:T(8,128)S(1)} %broadcast_in_dim.8), channel_id=1, replica_groups={{0,2,4,6,8,10,12,14},{1,3,5,7,9,11,13,15},{16,18,20,22,24,26,28,30},{17..., dimensions={0} | all-to-all | bytes 458752 | tf_op jit(solution)/shard_map/all_to_all | solution.py:67
  66.0 0.0 collective-permute-start.1
  66.0 1.5 %collective-permute-done.1 = f32[448,128]{1,0:T(8,128)S(1)} collective-permute-done((f32[448,128]{1,0:T(8,128)S(1)}, f32[448,128]{1,0:T(8,128)S(1)}, u32[]{:S(2)}, u32[]{:S(2)}) %collective-permute-start.1) | collective-permute-done | bytes 229408 | tf_op jit(solution)/shard_map/ppermute | solution.py:68
  67.5 1.0 fusion.5
  68.6 2.4 %fusion.2 = f32[256,1152]{1,0:T(8,128)S(1)} fusion(f32[448,1152]{1,0:T(8,128)S(1)} %copy-done.1, bf16[448,1152]{1,0:T(8,128)(2,1)S(1)} %copy-done.2, f32[448,128]{1,0:T(8,128)S(1)} %collective-permute-done.1, f32[448,128]{1,0:T(8,128)S(1)} %bitcast.16, pred[]{:T(512)S(6)} %eq.17), kind=kOutput, calls=%fused_computation.6 | convolution fusion | flops 1586823168 | bytes 4734977 | tf_op jit(solution)/shard_map/dot_general | solution.py:42
  71.0 0.2 pad_maximum_fusion
  71.2 26.7 %all_to_all.32.parts_ref = f32[16,16,1536]{2,1,0:T(8,128)S(1)} all-to-all(f32[16,16,1536]{2,1,0:T(8,128)S(1)} %pad_maximum_fusion), channel_id=1, replica_groups=mesh['row'=16,'col'=16] {'row'}, dimensions={0} | all-to-all | bytes 3145728 | tf_op jit(solution)/shard_map/all_to_all | solution.py:298
  97.8 1.1 shard_map.68
  98.9 5.9 %all-to-all-start.4 = ((f32[16,16,1152]{2,1,0:T(8,128)}), f32[16,16,1152]{2,1,0:T(8,128)S(1)}, u32[]{:S(2)}, u32[]{:S(2)}) async-start(f32[16,16,1152]{2,1,0:T(8,128)} %get-tuple-element.14), calls=%async_computation.4 | async-start | bytes 2359296 | tf_op jit(solution)/shard_map/all_to_all | solution.py:49
  104.8 0.5 collective-permute-start.2
  105.4 3.3 %collective-permute-done.2 = f32[16,384]{1,0:T(8,128)S(1)} collective-permute-done((f32[16,384]{1,0:T(8,128)S(1)}, f32[16,384]{1,0:T(8,128)S(1)}, u32[]{:S(2)}, u32[]{:S(2)}) %collective-permute-start.2) | collective-permute-done | bytes 24608 | tf_op jit(solution)/shard_map/ppermute | solution.py:86
  108.7 0.5 collective-permute-start.3
  109.1 4.8 %collective-permute-done.3 = f32[32,384]{1,0:T(8,128)S(1)} collective-permute-done((f32[32,384]{1,0:T(8,128)S(1)}, f32[32,384]{1,0:T(8,128)S(1)}, u32[]{:S(2)}, u32[]{:S(2)}) %collective-permute-start.3) | collective-permute-done | bytes 49184 | tf_op jit(solution)/shard_map/ppermute | solution.py:88
  114.0 0.3 collective-permute-start.4
  114.3 1.3 collective-permute-done.4
  115.6 7.0 %shard_map.69.inverse_ref = f32[256,256]{1,0:T(8,128)S(1)} custom-call(f32[128,384]{1,0:T(8,128)S(1)} %maximum_select_fusion.1.gram_ref), custom_call_target="tpu_custom_call" | custom-call | flops 33554432 | bytes 524288 | tf_op jit(solution)/shard_map/pallas_call | solution.py:180
  122.6 0.0 all-to-all-done.4
  122.6 2.2 %shard_map.70 = (f32[256,1152]{1,0:T(8,128)S(1)}, f32[1,256]{1,0:T(1,128)S(1)}) custom-call(f32[256,256]{1,0:T(8,128)S(1)} %shard_map.69.inverse_ref, f32[256,1152]{1,0:T(8,128)S(1)} %bitcast.12), custom_call_target="tpu_custom_call" | custom-call | flops 905969664 | bytes 2359296 | tf_op jit(solution)/shard_map/pallas_call | solution.py:216
  124.8 0.2 collective-permute-start.5
  125.1 0.6 fusion.4
  125.6 0.4 collective-permute-done.5
  126.1 0.6 broadcast_in_dim.11
  126.7 3.3 %all-to-all-start.5 = ((f32[8,1,256]{2,1,0:T(1,128)}), f32[8,1,256]{2,1,0:T(1,128)S(1)}, u32[]{:S(2)}, u32[]{:S(2)}) async-start(f32[8,1,256]{2,1,0:T(1,128)} %broadcast_in_dim.11), calls=%async_computation.5 | async-start | bytes 16384 | tf_op jit(solution)/shard_map/all_to_all | solution.py:95
  130.0 4.4 %fusion.1 = f32[448,1152]{1,0:T(8,128)} fusion(f32[448,256]{1,0:T(8,128)S(1)} %fusion.4, f32[256,1152]{1,0:T(8,128)S(1)} %get-tuple-element.15, f32[448,1152]{1,0:T(8,128)} %param.4, bf16[448,1152]{1,0:T(8,128)(2,1)} %param.5), kind=kOutput, calls=%fused_computation.3 | convolution fusion | flops 794787840 | bytes 6799360 | tf_op jit(solution)/shard_map/dot_general | solution.py:42
  134.4 3.3 %all-to-all-done.5 = f32[8,1,256]{2,1,0:T(1,128)S(1)} async-done(((f32[8,1,256]{2,1,0:T(1,128)}), f32[8,1,256]{2,1,0:T(1,128)S(1)}, u32[]{:S(2)}, u32[]{:S(2)}) %all-to-all-start.5) | async-done | bytes 8224 | tf_op jit(solution)/shard_map/all_to_all | solution.py:95
  137.7 0.0 copy-start.3
  137.7 0.1 broadcast_multiply_fusion
  137.9 0.6 constant_dynamic-slice_fusion
  138.5 0.8 copy-done.3
  139.3 2.6 %fusion = f32[448,1152]{1,0:T(8,128)} fusion(f32[448,256]{1,0:T(8,128)S(1)} %fusion.4, f32[256,1152]{1,0:T(8,128)S(1)} %broadcast_multiply_fusion, f32[448,1152]{1,0:T(8,128)S(1)} %copy-done.3), kind=kOutput, calls=%fused_computation.1 | convolution fusion | flops 794271744 | bytes 5767168 | tf_op jit(solution)/shard_map/dot_general | solution.py:42
  (12 shorter events, 0.2 us)
Async XLA Ops:
  0.6 0.9 copy-start
  1.5 25.3 %copy-start.1 = (f32[448,1152]{1,0:T(8,128)S(1)}, f32[448,1152]{1,0:T(8,128)}, u32[]{:S(2)}) copy-start(f32[448,1152]{1,0:T(8,128)} %param.4) | copy-start | bytes 6193156
  1.5 25.3 %copy-start.2 = (bf16[448,1152]{1,0:T(8,128)(2,1)S(1)}, bf16[448,1152]{1,0:T(8,128)(2,1)}, u32[]{:S(2)}) copy-start(bf16[448,1152]{1,0:T(8,128)(2,1)} %param.5) | copy-start | bytes 3096580
  2.6 24.2 %all-to-all-start = ((f32[16,16,1152]{2,1,0:T(8,128)}), f32[16,16,1152]{2,1,0:T(8,128)}, u32[]{:S(2)}, u32[]{:S(2)}) async-start(f32[16,16,1152]{2,1,0:T(8,128)} %shard_map.67), calls=%async_computation | async-start | bytes 2359296 | tf_op jit(solution)/shard_map/all_to_all | solution.py:49
  30.8 1.8 %collective-permute-start = (f32[448,128]{1,0:T(8,128)}, f32[448,128]{1,0:T(8,128)}, u32[]{:S(2)}, u32[]{:S(2)}) collective-permute-start(f32[448,128]{1,0:T(8,128)} %constant_dynamic-slice_fusion.2), channel_id=1, source_target_pairs={{0,1},{1,0},{2,3},{3,2},{4,5},{5,4},{6,7},{7,6},{8,9},{9,8},{10,11... | collective-permute-start | bytes 688136 | tf_op jit(solution)/shard_map/ppermute | solution.py:63
  66.0 1.5 %collective-permute-start.1 = (f32[448,128]{1,0:T(8,128)S(1)}, f32[448,128]{1,0:T(8,128)S(1)}, u32[]{:S(2)}, u32[]{:S(2)}) collective-permute-start(f32[448,128]{1,0:T(8,128)S(1)} %bitcast.14), channel_id=1, source_target_pairs={{0,1},{1,0},{2,3},{3,2},{4,5},{5,4},{6,7},{7,6},{8,9},{9,8},{10,11... | collective-permute-start | bytes 688136 | tf_op jit(solution)/shard_map/ppermute | solution.py:68
  98.9 23.7 %all-to-all-start.4 = ((f32[16,16,1152]{2,1,0:T(8,128)}), f32[16,16,1152]{2,1,0:T(8,128)S(1)}, u32[]{:S(2)}, u32[]{:S(2)}) async-start(f32[16,16,1152]{2,1,0:T(8,128)} %get-tuple-element.14), calls=%async_computation.4 | async-start | bytes 2359296 | tf_op jit(solution)/shard_map/all_to_all | solution.py:49
  104.8 3.8 %collective-permute-start.2 = (f32[16,384]{1,0:T(8,128)S(1)}, f32[16,384]{1,0:T(8,128)S(1)}, u32[]{:S(2)}, u32[]{:S(2)}) collective-permute-start(f32[16,384]{1,0:T(8,128)S(1)} %get-tuple-element.13), channel_id=1, source_target_pairs={{0,2},{1,3},{2,0},{3,1},{4,6},{5,7},{6,4},{7,5},{8,10},{9,11},{10,... | collective-permute-start | bytes 73736 | tf_op jit(solution)/shard_map/ppermute | solution.py:86
  108.7 5.3 %collective-permute-start.3 = (f32[32,384]{1,0:T(8,128)S(1)}, f32[32,384]{1,0:T(8,128)S(1)}, u32[]{:S(2)}, u32[]{:S(2)}) collective-permute-start(f32[32,384]{1,0:T(8,128)S(1)} %maximum_select_fusion.6), channel_id=1, source_target_pairs={{0,14},{1,15},{2,4},{3,5},{4,2},{5,3},{6,8},{7,9},{8,6},{9,7},{10,... | collective-permute-start | bytes 147464 | tf_op jit(solution)/shard_map/ppermute | solution.py:88
  114.0 1.6 %collective-permute-start.4 = (f32[64,384]{1,0:T(8,128)S(1)}, f32[64,384]{1,0:T(8,128)S(1)}, u32[]{:S(2)}, u32[]{:S(2)}) collective-permute-start(f32[64,384]{1,0:T(8,128)S(1)} %maximum_select_fusion.2), channel_id=1, source_target_pairs={{0,1},{1,0},{2,3},{3,2},{4,5},{5,4},{6,7},{7,6},{8,9},{9,8},{10,11... | collective-permute-start | bytes 294920 | tf_op jit(solution)/shard_map/ppermute | solution.py:89
  124.8 1.2 collective-permute-start.5
  126.7 11.0 %all-to-all-start.5 = ((f32[8,1,256]{2,1,0:T(1,128)}), f32[8,1,256]{2,1,0:T(1,128)S(1)}, u32[]{:S(2)}, u32[]{:S(2)}) async-start(f32[8,1,256]{2,1,0:T(1,128)} %broadcast_in_dim.11), calls=%async_computation.5 | async-start | bytes 16384 | tf_op jit(solution)/shard_map/all_to_all | solution.py:95
  137.7 1.6 %copy-start.3 = (f32[448,1152]{1,0:T(8,128)S(1)}, f32[448,1152]{1,0:T(8,128)}, u32[]{:S(2)}) copy-start(f32[448,1152]{1,0:T(8,128)} %param.6) | copy-start | bytes 6193156

commit v6 on v5

--- a/solution.py
+++ b/solution.py
@@ -188,41 +188,28 @@
     )(packed)
 
 
-def right_product_kernel(inverse_ref, cross_ref, out_ref, squares_ref, total):
-    step = pl.program_id(0)
-    value = product(inverse_ref[...], cross_ref[...], ((1,), (0,)))
-    out_ref[...] = value
-    squared = value * value
-    tiles = [squared[:, LANES * t : LANES * (t + 1)] for t in range(value.shape[1] // LANES)]
-
-    @pl.when(step == 0)
-    def _():
-        total[...] = sum(tiles)
-
-    @pl.when(step > 0)
-    def _():
-        total[...] += sum(tiles)
-
-    @pl.when(step == pl.num_programs(0) - 1)
-    def _():
-        squares_ref[...] = jnp.sum(total[...].T, axis=0, keepdims=True)
+def right_product_kernel(inverse_ref, cross_ref, out_ref, squares_ref):
+    inverse = inverse_ref[...]
+    total = jnp.zeros((inverse.shape[0], LANES), jnp.float32)
+    for start in range(0, cross_ref.shape[1], 3 * LANES):
+        value = product(inverse, cross_ref[:, start : start + 3 * LANES], ((1,), (0,)))
+        out_ref[:, start : start + 3 * LANES] = value
+        for at in range(0, 3 * LANES, LANES):
+            total += value[:, at : at + LANES] * value[:, at : at + LANES]
+    squares_ref[...] = jnp.sum(total.T, axis=0, keepdims=True)
 
 
 def right_product_and_squares(inverse, cross):
     rank, columns = cross.shape
-    block = 3 * LANES
-    whole = pl.BlockSpec((rank, rank), lambda i: (0, 0))
-    strip = pl.BlockSpec((rank, block), lambda i: (0, i))
+    vmem = pl.BlockSpec(memory_space=pltpu.VMEM)
     return pl.pallas_call(
         right_product_kernel,
-        grid=(columns // block,),
         out_shape=(
             jax.ShapeDtypeStruct(cross.shape, jnp.float32),
             jax.ShapeDtypeStruct((1, rank), jnp.float32),
         ),
-        in_specs=[whole, strip],
-        out_specs=(strip, pl.BlockSpec((1, rank), lambda i: (0, 0))),
-        scratch_shapes=[pltpu.VMEM((rank, LANES), jnp.float32)],
+        in_specs=[vmem, vmem],
+        out_specs=(vmem, vmem),
         compiler_params=pltpu.CompilerParams(vmem_limit_bytes=8 * 2**20),
         cost_estimate=pl.CostEstimate(
             flops=12 * rank * rank * columns, bytes_accessed=8 * cross.size, transcendentals=0

time: 143 us -> 142 us (level)
  transfers between devices with their start and end apart: 9 -> 9, of which waited for: 8 -> 8; matrix products, arithmetic and copies ran while one was open for 3% -> 4% of each run, Pallas kernels for 5% -> 5%
where the time goes in v6:
time: 142 us; the launch traced here: 141 us
  blocking collectives  59 us (42%)
  waiting for transfers between devices  33.1 us (23%)
  starting transfers between devices  18.3 us (13%)
  matrix products  14.2 us (10%)
  Pallas kernels  10.7 us (8%)
  local copies, waits for them, and re-layouts  3.71 us (3%)
    all_to_all x1, blocking collectives, per_device(): taken = lax.all_to_all(parts, 'row', 0, 0)  26.7 us
    all_to_all x1, blocking collectives, sum_over_col(): lax.all_to_all(parts, 'col', 0, 0, axis_index_groups=Z_GROUPS)  19.7 us
    all_to_all x2, waiting for transfers between devices, gather_over_row(): lax.all_to_all(copies, 'row', 0, 0)  16.6 us
    dot_general x6, matrix products, product(): lax.dot_general(a, b, (contract, ((), ())), precision=precision, preferre...  14.2 us
    all_to_all x2, starting transfers between devices, gather_over_row(): lax.all_to_all(copies, 'row', 0, 0)  13.5 us
    all_to_all x1, blocking collectives, sum_over_col(): lax.all_to_all(copies, 'col', 0, 0, axis_index_groups=Z_GROUPS)  12.6 us
    pallas_call x1, Pallas kernels, inverse_factor(): pl.pallas_call(inverse_factor_kernel, out_shape=jax.ShapeDtypeStruct((n,...  7.03 us
    ppermute x1, waiting for transfers between devices, gather_bands(): lax.ppermute(mine, 'col', Z_BUTTERFLY[1])  4.84 us
  transfers between devices with their start and end apart: 9, of which 8 were waited for; matrix products, arithmetic and copies ran while one was open for 4% of the time, Pallas kernels for 5%

profile of v6, /device:TPU:2, one launch (start us, length us, event | category | flops | bytes accessed | tf_op | source)
XLA Modules:
  0.0 141.2 jit_solution(8552472724785405633)
XLA Ops:
  0.6 0.0 copy-start
  0.6 0.9 copy-done
  1.5 0.0 copy-start.1
  1.5 0.0 copy-start.2
  1.5 1.1 shard_map.67
  2.6 7.6 %all-to-all-start = ((f32[16,16,1152]{2,1,0:T(8,128)}), f32[16,16,1152]{2,1,0:T(8,128)}, u32[]{:S(2)}, u32[]{:S(2)}) async-start(f32[16,16,1152]{2,1,0:T(8,128)} %shard_map.67), calls=%async_computation | async-start | bytes 2359296 | tf_op jit(solution)/shard_map/all_to_all | solution.py:49
  10.2 16.6 %all-to-all-done = f32[16,16,1152]{2,1,0:T(8,128)} async-done(((f32[16,16,1152]{2,1,0:T(8,128)}), f32[16,16,1152]{2,1,0:T(8,128)}, u32[]{:S(2)}, u32[]{:S(2)}) %all-to-all-start) | async-done | bytes 1179680 | tf_op jit(solution)/shard_map/all_to_all | solution.py:49
  26.8 0.0 copy-done.1
  26.8 0.0 copy-done.2
  26.8 3.3 %fusion.3 = f32[448,256]{1,0:T(8,128)S(1)} fusion(f32[256,1152]{1,0:T(8,128)} %bitcast, f32[448,1152]{1,0:T(8,128)S(1)} %copy-done.1, bf16[448,1152]{1,0:T(8,128)(2,1)S(1)} %copy-done.2), kind=kOutput, calls=%fused_computation.7 | convolution fusion | flops 1586479104 | bytes 4734976 | tf_op jit(solution)/shard_map/dot_general | solution.py:42
  30.1 0.7 constant_dynamic-slice_fusion.2
  30.8 0.0 collective-permute-start
  30.8 1.8 %collective-permute-done = f32[448,128]{1,0:T(8,128)} collective-permute-done((f32[448,128]{1,0:T(8,128)}, f32[448,128]{1,0:T(8,128)}, u32[]{:S(2)}, u32[]{:S(2)}) %collective-permute-start) | collective-permute-done | bytes 229408 | tf_op jit(solution)/shard_map/ppermute | solution.py:63
  32.6 1.0 dynamic-slice_add_fusion
  33.6 19.7 %all_to_all.30 = f32[8,56,128]{2,1,0:T(8,128)S(1)} all-to-all(f32[8,56,128]{2,1,0:T(8,128)S(1)} %bitcast.18), channel_id=1, replica_groups={{0,2,4,6,8,10,12,14},{1,3,5,7,9,11,13,15},{16,18,20,22,24,26,28,30},{17..., dimensions={0} | all-to-all | bytes 458752 | tf_op jit(solution)/shard_map/all_to_all | solution.py:65
  53.4 12.6 %all_to_all.31 = f32[8,56,128]{2,1,0:T(8,128)S(1)} all-to-all(f32[8,56,128]{2,1,0:T(8,128)S(1)} %broadcast_in_dim.8), channel_id=1, replica_groups={{0,2,4,6,8,10,12,14},{1,3,5,7,9,11,13,15},{16,18,20,22,24,26,28,30},{17..., dimensions={0} | all-to-all | bytes 458752 | tf_op jit(solution)/shard_map/all_to_all | solution.py:67
  66.0 0.0 collective-permute-start.1
  66.0 1.5 %collective-permute-done.1 = f32[448,128]{1,0:T(8,128)S(1)} collective-permute-done((f32[448,128]{1,0:T(8,128)S(1)}, f32[448,128]{1,0:T(8,128)S(1)}, u32[]{:S(2)}, u32[]{:S(2)}) %collective-permute-start.1) | collective-permute-done | bytes 229408 | tf_op jit(solution)/shard_map/ppermute | solution.py:68
  67.5 1.0 fusion.5
  68.6 2.4 %fusion.2 = f32[256,1152]{1,0:T(8,128)S(1)} fusion(f32[448,1152]{1,0:T(8,128)S(1)} %copy-done.1, bf16[448,1152]{1,0:T(8,128)(2,1)S(1)} %copy-done.2, f32[448,128]{1,0:T(8,128)S(1)} %collective-permute-done.1, f32[448,128]{1,0:T(8,128)S(1)} %bitcast.16, pred[]{:T(512)S(6)} %eq.17), kind=kOutput, calls=%fused_computation.6 | convolution fusion | flops 1586823168 | bytes 4734977 | tf_op jit(solution)/shard_map/dot_general | solution.py:42
  71.0 0.2 pad_maximum_fusion
  71.2 26.7 %all_to_all.32.parts_ref = f32[16,16,1536]{2,1,0:T(8,128)S(1)} all-to-all(f32[16,16,1536]{2,1,0:T(8,128)S(1)} %pad_maximum_fusion), channel_id=1, replica_groups=mesh['row'=16,'col'=16] {'row'}, dimensions={0} | all-to-all | bytes 3145728 | tf_op jit(solution)/shard_map/all_to_all | solution.py:285
  97.8 1.1 shard_map.68
  98.9 5.9 %all-to-all-start.4 = ((f32[16,16,1152]{2,1,0:T(8,128)}), f32[16,16,1152]{2,1,0:T(8,128)S(1)}, u32[]{:S(2)}, u32[]{:S(2)}) async-start(f32[16,16,1152]{2,1,0:T(8,128)} %get-tuple-element.14), calls=%async_computation.4 | async-start | bytes 2359296 | tf_op jit(solution)/shard_map/all_to_all | solution.py:49
  104.8 0.5 collective-permute-start.2
  105.4 3.3 %collective-permute-done.2 = f32[16,384]{1,0:T(8,128)S(1)} collective-permute-done((f32[16,384]{1,0:T(8,128)S(1)}, f32[16,384]{1,0:T(8,128)S(1)}, u32[]{:S(2)}, u32[]{:S(2)}) %collective-permute-start.2) | collective-permute-done | bytes 24608 | tf_op jit(solution)/shard_map/ppermute | solution.py:86
  108.7 0.5 collective-permute-start.3
  109.1 4.8 %collective-permute-done.3 = f32[32,384]{1,0:T(8,128)S(1)} collective-permute-done((f32[32,384]{1,0:T(8,128)S(1)}, f32[32,384]{1,0:T(8,128)S(1)}, u32[]{:S(2)}, u32[]{:S(2)}) %collective-permute-start.3) | collective-permute-done | bytes 49184 | tf_op jit(solution)/shard_map/ppermute | solution.py:88
  114.0 0.3 collective-permute-start.4
  114.3 1.3 collective-permute-done.4
  115.6 7.0 %shard_map.69.inverse_ref = f32[256,256]{1,0:T(8,128)S(1)} custom-call(f32[128,384]{1,0:T(8,128)S(1)} %maximum_select_fusion.1.gram_ref), custom_call_target="tpu_custom_call" | custom-call | flops 33554432 | bytes 524288 | tf_op jit(solution)/shard_map/pallas_call | solution.py:180
  122.6 0.0 all-to-all-done.4
  122.6 1.5 %shard_map.70 = (f32[256,1152]{1,0:T(8,128)S(1)}, f32[1,256]{1,0:T(1,128)S(1)}) custom-call(f32[256,256]{1,0:T(8,128)S(1)} %shard_map.69.inverse_ref, f32[256,1152]{1,0:T(8,128)S(1)} %bitcast.12), custom_call_target="tpu_custom_call" | custom-call | flops 905969664 | bytes 2359296 | tf_op jit(solution)/shard_map/pallas_call | solution.py:205
  124.1 0.2 collective-permute-start.5
  124.4 0.6 fusion.4
  124.9 0.4 collective-permute-done.5
  125.3 0.6 broadcast_in_dim.11
  125.9 3.3 %all-to-all-start.5 = ((f32[8,1,256]{2,1,0:T(1,128)}), f32[8,1,256]{2,1,0:T(1,128)S(1)}, u32[]{:S(2)}, u32[]{:S(2)}) async-start(f32[8,1,256]{2,1,0:T(1,128)} %broadcast_in_dim.11), calls=%async_computation.5 | async-start | bytes 16384 | tf_op jit(solution)/shard_map/all_to_all | solution.py:95
  129.3 4.4 %fusion.1 = f32[448,1152]{1,0:T(8,128)} fusion(f32[448,256]{1,0:T(8,128)S(1)} %fusion.4, f32[256,1152]{1,0:T(8,128)S(1)} %get-tuple-element.15, f32[448,1152]{1,0:T(8,128)} %param.4, bf16[448,1152]{1,0:T(8,128)(2,1)} %param.5), kind=kOutput, calls=%fused_computation.3 | convolution fusion | flops 794787840 | bytes 6799360 | tf_op jit(solution)/shard_map/dot_general | solution.py:42
  133.7 3.3 %all-to-all-done.5 = f32[8,1,256]{2,1,0:T(1,128)S(1)} async-done(((f32[8,1,256]{2,1,0:T(1,128)}), f32[8,1,256]{2,1,0:T(1,128)S(1)}, u32[]{:S(2)}, u32[]{:S(2)}) %all-to-all-start.5) | async-done | bytes 8224 | tf_op jit(solution)/shard_map/all_to_all | solution.py:95
  137.0 0.0 copy-start.3
  137.0 0.1 broadcast_multiply_fusion
  137.2 0.6 constant_dynamic-slice_fusion
  137.8 0.8 copy-done.3
  138.6 2.6 %fusion = f32[448,1152]{1,0:T(8,128)} fusion(f32[448,256]{1,0:T(8,128)S(1)} %fusion.4, f32[256,1152]{1,0:T(8,128)S(1)} %broadcast_multiply_fusion, f32[448,1152]{1,0:T(8,128)S(1)} %copy-done.3), kind=kOutput, calls=%fused_computation.1 | convolution fusion | flops 794271744 | bytes 5767168 | tf_op jit(solution)/shard_map/dot_general | solution.py:42
  (12 shorter events, 0.2 us)
Async XLA Ops:
  0.6 0.9 copy-start
  1.5 25.3 %copy-start.1 = (f32[448,1152]{1,0:T(8,128)S(1)}, f32[448,1152]{1,0:T(8,128)}, u32[]{:S(2)}) copy-start(f32[448,1152]{1,0:T(8,128)} %param.4) | copy-start | bytes 6193156
  1.5 25.3 %copy-start.2 = (bf16[448,1152]{1,0:T(8,128)(2,1)S(1)}, bf16[448,1152]{1,0:T(8,128)(2,1)}, u32[]{:S(2)}) copy-start(bf16[448,1152]{1,0:T(8,128)(2,1)} %param.5) | copy-start | bytes 3096580
  2.6 24.2 %all-to-all-start = ((f32[16,16,1152]{2,1,0:T(8,128)}), f32[16,16,1152]{2,1,0:T(8,128)}, u32[]{:S(2)}, u32[]{:S(2)}) async-start(f32[16,16,1152]{2,1,0:T(8,128)} %shard_map.67), calls=%async_computation | async-start | bytes 2359296 | tf_op jit(solution)/shard_map/all_to_all | solution.py:49
  30.8 1.8 %collective-permute-start = (f32[448,128]{1,0:T(8,128)}, f32[448,128]{1,0:T(8,128)}, u32[]{:S(2)}, u32[]{:S(2)}) collective-permute-start(f32[448,128]{1,0:T(8,128)} %constant_dynamic-slice_fusion.2), channel_id=1, source_target_pairs={{0,1},{1,0},{2,3},{3,2},{4,5},{5,4},{6,7},{7,6},{8,9},{9,8},{10,11... | collective-permute-start | bytes 688136 | tf_op jit(solution)/shard_map/ppermute | solution.py:63
  66.0 1.5 %collective-permute-start.1 = (f32[448,128]{1,0:T(8,128)S(1)}, f32[448,128]{1,0:T(8,128)S(1)}, u32[]{:S(2)}, u32[]{:S(2)}) collective-permute-start(f32[448,128]{1,0:T(8,128)S(1)} %bitcast.14), channel_id=1, source_target_pairs={{0,1},{1,0},{2,3},{3,2},{4,5},{5,4},{6,7},{7,6},{8,9},{9,8},{10,11... | collective-permute-start | bytes 688136 | tf_op jit(solution)/shard_map/ppermute | solution.py:68
  98.9 23.7 %all-to-all-start.4 = ((f32[16,16,1152]{2,1,0:T(8,128)}), f32[16,16,1152]{2,1,0:T(8,128)S(1)}, u32[]{:S(2)}, u32[]{:S(2)}) async-start(f32[16,16,1152]{2,1,0:T(8,128)} %get-tuple-element.14), calls=%async_computation.4 | async-start | bytes 2359296 | tf_op jit(solution)/shard_map/all_to_all | solution.py:49
  104.8 3.8 %collective-permute-start.2 = (f32[16,384]{1,0:T(8,128)S(1)}, f32[16,384]{1,0:T(8,128)S(1)}, u32[]{:S(2)}, u32[]{:S(2)}) collective-permute-start(f32[16,384]{1,0:T(8,128)S(1)} %get-tuple-element.13), channel_id=1, source_target_pairs={{0,2},{1,3},{2,0},{3,1},{4,6},{5,7},{6,4},{7,5},{8,10},{9,11},{10,... | collective-permute-start | bytes 73736 | tf_op jit(solution)/shard_map/ppermute | solution.py:86
  108.7 5.3 %collective-permute-start.3 = (f32[32,384]{1,0:T(8,128)S(1)}, f32[32,384]{1,0:T(8,128)S(1)}, u32[]{:S(2)}, u32[]{:S(2)}) collective-permute-start(f32[32,384]{1,0:T(8,128)S(1)} %maximum_select_fusion.6), channel_id=1, source_target_pairs={{0,14},{1,15},{2,4},{3,5},{4,2},{5,3},{6,8},{7,9},{8,6},{9,7},{10,... | collective-permute-start | bytes 147464 | tf_op jit(solution)/shard_map/ppermute | solution.py:88
  114.0 1.6 %collective-permute-start.4 = (f32[64,384]{1,0:T(8,128)S(1)}, f32[64,384]{1,0:T(8,128)S(1)}, u32[]{:S(2)}, u32[]{:S(2)}) collective-permute-start(f32[64,384]{1,0:T(8,128)S(1)} %maximum_select_fusion.2), channel_id=1, source_target_pairs={{0,1},{1,0},{2,3},{3,2},{4,5},{5,4},{6,7},{7,6},{8,9},{9,8},{10,11... | collective-permute-start | bytes 294920 | tf_op jit(solution)/shard_map/ppermute | solution.py:89
  124.1 1.2 collective-permute-start.5
  125.9 11.0 %all-to-all-start.5 = ((f32[8,1,256]{2,1,0:T(1,128)}), f32[8,1,256]{2,1,0:T(1,128)S(1)}, u32[]{:S(2)}, u32[]{:S(2)}) async-start(f32[8,1,256]{2,1,0:T(1,128)} %broadcast_in_dim.11), calls=%async_computation.5 | async-start | bytes 16384 | tf_op jit(solution)/shard_map/all_to_all | solution.py:95
  137.0 1.6 %copy-start.3 = (f32[448,1152]{1,0:T(8,128)S(1)}, f32[448,1152]{1,0:T(8,128)}, u32[]{:S(2)}) copy-start(f32[448,1152]{1,0:T(8,128)} %param.6) | copy-start | bytes 6193156

commit v7 on v6

--- a/solution.py
+++ b/solution.py
@@ -58,8 +58,8 @@
     core = lax.axis_index("col") % 2
     rows, columns = whole.shape
     half = columns // 2
-    kept = lax.dynamic_slice_in_dim(whole, core * half, half, 1)
-    given = lax.dynamic_slice_in_dim(whole, (1 - core) * half, half, 1)
+    first, second = whole[:, :half], whole[:, half:]
+    kept, given = jnp.where(core == 0, first, second), jnp.where(core == 0, second, first)
     chip = kept + lax.ppermute(given, "col", CORE_SWAP)
     parts = chip.reshape(DEPTH, rows // DEPTH, half)
     part = jnp.sum(lax.all_to_all(parts, "col", 0, 0, axis_index_groups=Z_GROUPS), axis=0)

time: 142 us -> 140 us (0.986)
  no operation moved by 1% of the time
where the time goes in v7:
time: 140 us; the launch traced here: 139 us
  blocking collectives  59 us (42%)
  waiting for transfers between devices  32.7 us (23%)
  starting transfers between devices  18.4 us (13%)
  matrix products  14.2 us (10%)
  Pallas kernels  10.7 us (8%)
  local copies, waits for them, and re-layouts  3 us (2%)
    all_to_all x1, blocking collectives, per_device(): taken = lax.all_to_all(parts, 'row', 0, 0)  26.7 us
    all_to_all x1, blocking collectives, sum_over_col(): lax.all_to_all(parts, 'col', 0, 0, axis_index_groups=Z_GROUPS)  19.7 us
    all_to_all x2, waiting for transfers between devices, gather_over_row(): lax.all_to_all(copies, 'row', 0, 0)  16.6 us
    dot_general x6, matrix products, product(): lax.dot_general(a, b, (contract, ((), ())), precision=precision, preferre...  14.2 us
    all_to_all x2, starting transfers between devices, gather_over_row(): lax.all_to_all(copies, 'row', 0, 0)  13.5 us
    all_to_all x1, blocking collectives, sum_over_col(): lax.all_to_all(copies, 'col', 0, 0, axis_index_groups=Z_GROUPS)  12.6 us
    pallas_call x1, Pallas kernels, inverse_factor(): pl.pallas_call(inverse_factor_kernel, out_shape=jax.ShapeDtypeStruct((n,...  7.03 us
    ppermute x1, waiting for transfers between devices, gather_bands(): lax.ppermute(mine, 'col', Z_BUTTERFLY[1])  4.83 us
  transfers between devices with their start and end apart: 9, of which 8 were waited for; matrix products, arithmetic and copies ran while one was open for 4% of the time, Pallas kernels for 5%

profile of v7, /device:TPU:2, one launch (start us, length us, event | category | flops | bytes accessed | tf_op | source)
XLA Modules:
  0.0 139.4 jit_solution(2637288752692691281)
XLA Ops:
  0.6 0.0 copy-start
  0.6 0.9 copy-done
  1.5 0.0 copy-start.1
  1.5 0.0 copy-start.2
  1.5 1.1 shard_map.67
  2.6 7.6 %all-to-all-start = ((f32[16,16,1152]{2,1,0:T(8,128)}), f32[16,16,1152]{2,1,0:T(8,128)}, u32[]{:S(2)}, u32[]{:S(2)}) async-start(f32[16,16,1152]{2,1,0:T(8,128)} %shard_map.67), calls=%async_computation | async-start | bytes 2359296 | tf_op jit(solution)/shard_map/all_to_all | solution.py:49
  10.2 16.6 %all-to-all-done = f32[16,16,1152]{2,1,0:T(8,128)} async-done(((f32[16,16,1152]{2,1,0:T(8,128)}), f32[16,16,1152]{2,1,0:T(8,128)}, u32[]{:S(2)}, u32[]{:S(2)}) %all-to-all-start) | async-done | bytes 1179680 | tf_op jit(solution)/shard_map/all_to_all | solution.py:49
  26.8 0.0 copy-done.1
  26.8 0.0 copy-done.2
  26.8 3.3 %fusion.3 = f32[448,256]{1,0:T(8,128)S(1)} fusion(f32[256,1152]{1,0:T(8,128)} %bitcast, f32[448,1152]{1,0:T(8,128)S(1)} %copy-done.1, bf16[448,1152]{1,0:T(8,128)(2,1)S(1)} %copy-done.2), kind=kOutput, calls=%fused_computation.7 | convolution fusion | flops 1586479104 | bytes 4734976 | tf_op jit(solution)/shard_map/dot_general | solution.py:42
  30.1 0.1 collective-permute-start
  30.2 1.5 %collective-permute-done = f32[448,128]{1,0:T(8,128)S(1)} collective-permute-done((f32[448,128]{1,0:T(8,128)S(1)}, f32[448,128]{1,0:T(8,128)S(1)}, u32[]{:S(2)}, u32[]{:S(2)}) %collective-permute-start) | collective-permute-done | bytes 229408 | tf_op jit(solution)/shard_map/ppermute | solution.py:63
  31.7 0.1 select_add_fusion
  31.7 19.7 %all_to_all.30 = f32[8,56,128]{2,1,0:T(8,128)S(1)} all-to-all(f32[8,56,128]{2,1,0:T(8,128)S(1)} %bitcast.18), channel_id=1, replica_groups={{0,2,4,6,8,10,12,14},{1,3,5,7,9,11,13,15},{16,18,20,22,24,26,28,30},{17..., dimensions={0} | all-to-all | bytes 458752 | tf_op jit(solution)/shard_map/all_to_all | solution.py:65
  51.5 12.6 %all_to_all.31 = f32[8,56,128]{2,1,0:T(8,128)S(1)} all-to-all(f32[8,56,128]{2,1,0:T(8,128)S(1)} %broadcast_in_dim.8), channel_id=1, replica_groups={{0,2,4,6,8,10,12,14},{1,3,5,7,9,11,13,15},{16,18,20,22,24,26,28,30},{17..., dimensions={0} | all-to-all | bytes 458752 | tf_op jit(solution)/shard_map/all_to_all | solution.py:67
  64.2 0.0 collective-permute-start.1
  64.2 1.5 %collective-permute-done.1 = f32[448,128]{1,0:T(8,128)S(1)} collective-permute-done((f32[448,128]{1,0:T(8,128)S(1)}, f32[448,128]{1,0:T(8,128)S(1)}, u32[]{:S(2)}, u32[]{:S(2)}) %collective-permute-start.1) | collective-permute-done | bytes 229408 | tf_op jit(solution)/shard_map/ppermute | solution.py:68
  65.6 1.0 fusion.5
  66.7 2.4 %fusion.2 = f32[256,1152]{1,0:T(8,128)S(1)} fusion(f32[448,1152]{1,0:T(8,128)S(1)} %copy-done.1, bf16[448,1152]{1,0:T(8,128)(2,1)S(1)} %copy-done.2, f32[448,128]{1,0:T(8,128)S(1)} %collective-permute-done.1, f32[448,128]{1,0:T(8,128)S(1)} %bitcast.16, pred[]{:T(512)S(6)} %eq.19), kind=kOutput, calls=%fused_computation.6 | convolution fusion | flops 1586823168 | bytes 4734977 | tf_op jit(solution)/shard_map/dot_general | solution.py:42
  69.1 0.2 pad_maximum_fusion
  69.3 26.7 %all_to_all.32.parts_ref = f32[16,16,1536]{2,1,0:T(8,128)S(1)} all-to-all(f32[16,16,1536]{2,1,0:T(8,128)S(1)} %pad_maximum_fusion), channel_id=1, replica_groups=mesh['row'=16,'col'=16] {'row'}, dimensions={0} | all-to-all | bytes 3145728 | tf_op jit(solution)/shard_map/all_to_all | solution.py:285
  96.0 1.1 shard_map.68
  97.1 5.9 %all-to-all-start.4 = ((f32[16,16,1152]{2,1,0:T(8,128)}), f32[16,16,1152]{2,1,0:T(8,128)S(1)}, u32[]{:S(2)}, u32[]{:S(2)}) async-start(f32[16,16,1152]{2,1,0:T(8,128)} %get-tuple-element.14), calls=%async_computation.4 | async-start | bytes 2359296 | tf_op jit(solution)/shard_map/all_to_all | solution.py:49
  103.0 0.5 collective-permute-start.2
  103.5 3.3 %collective-permute-done.2 = f32[16,384]{1,0:T(8,128)S(1)} collective-permute-done((f32[16,384]{1,0:T(8,128)S(1)}, f32[16,384]{1,0:T(8,128)S(1)}, u32[]{:S(2)}, u32[]{:S(2)}) %collective-permute-start.2) | collective-permute-done | bytes 24608 | tf_op jit(solution)/shard_map/ppermute | solution.py:86
  106.8 0.5 collective-permute-start.3
  107.3 4.8 %collective-permute-done.3 = f32[32,384]{1,0:T(8,128)S(1)} collective-permute-done((f32[32,384]{1,0:T(8,128)S(1)}, f32[32,384]{1,0:T(8,128)S(1)}, u32[]{:S(2)}, u32[]{:S(2)}) %collective-permute-start.3) | collective-permute-done | bytes 49184 | tf_op jit(solution)/shard_map/ppermute | solution.py:88
  112.1 0.3 collective-permute-start.4
  112.4 1.3 collective-permute-done.4
  113.7 7.0 %shard_map.69.inverse_ref = f32[256,256]{1,0:T(8,128)S(1)} custom-call(f32[128,384]{1,0:T(8,128)S(1)} %maximum_select_fusion.1.gram_ref), custom_call_target="tpu_custom_call" | custom-call | flops 33554432 | bytes 524288 | tf_op jit(solution)/shard_map/pallas_call | solution.py:180
  120.7 0.0 all-to-all-done.4
  120.8 1.5 %shard_map.70 = (f32[256,1152]{1,0:T(8,128)S(1)}, f32[1,256]{1,0:T(1,128)S(1)}) custom-call(f32[256,256]{1,0:T(8,128)S(1)} %shard_map.69.inverse_ref, f32[256,1152]{1,0:T(8,128)S(1)} %bitcast.12), custom_call_target="tpu_custom_call" | custom-call | flops 905969664 | bytes 2359296 | tf_op jit(solution)/shard_map/pallas_call | solution.py:205
  122.2 0.2 collective-permute-start.5
  122.5 0.6 fusion.4
  123.1 0.4 collective-permute-done.5
  123.5 0.6 broadcast_in_dim.11
  124.1 3.3 %all-to-all-start.5 = ((f32[8,1,256]{2,1,0:T(1,128)}), f32[8,1,256]{2,1,0:T(1,128)S(1)}, u32[]{:S(2)}, u32[]{:S(2)}) async-start(f32[8,1,256]{2,1,0:T(1,128)} %broadcast_in_dim.11), calls=%async_computation.5 | async-start | bytes 16384 | tf_op jit(solution)/shard_map/all_to_all | solution.py:95
  127.4 4.4 %fusion.1 = f32[448,1152]{1,0:T(8,128)} fusion(f32[448,256]{1,0:T(8,128)S(1)} %fusion.4, f32[256,1152]{1,0:T(8,128)S(1)} %get-tuple-element.15, f32[448,1152]{1,0:T(8,128)} %param.4, bf16[448,1152]{1,0:T(8,128)(2,1)} %param.5), kind=kOutput, calls=%fused_computation.3 | convolution fusion | flops 794787840 | bytes 6799360 | tf_op jit(solution)/shard_map/dot_general | solution.py:42
  131.8 3.3 %all-to-all-done.5 = f32[8,1,256]{2,1,0:T(1,128)S(1)} async-done(((f32[8,1,256]{2,1,0:T(1,128)}), f32[8,1,256]{2,1,0:T(1,128)S(1)}, u32[]{:S(2)}, u32[]{:S(2)}) %all-to-all-start.5) | async-done | bytes 8224 | tf_op jit(solution)/shard_map/all_to_all | solution.py:95
  135.1 0.0 copy-start.3
  135.1 0.1 broadcast_multiply_fusion
  135.3 0.6 constant_dynamic-slice_fusion
  135.9 0.8 copy-done.3
  136.7 2.6 %fusion = f32[448,1152]{1,0:T(8,128)} fusion(f32[448,256]{1,0:T(8,128)S(1)} %fusion.4, f32[256,1152]{1,0:T(8,128)S(1)} %broadcast_multiply_fusion, f32[448,1152]{1,0:T(8,128)S(1)} %copy-done.3), kind=kOutput, calls=%fused_computation.1 | convolution fusion | flops 794271744 | bytes 5767168 | tf_op jit(solution)/shard_map/dot_general | solution.py:42
  (13 shorter events, 0.2 us)
Async XLA Ops:
  0.6 0.9 copy-start
  1.5 25.3 %copy-start.1 = (f32[448,1152]{1,0:T(8,128)S(1)}, f32[448,1152]{1,0:T(8,128)}, u32[]{:S(2)}) copy-start(f32[448,1152]{1,0:T(8,128)} %param.4) | copy-start | bytes 6193156
  1.5 25.3 %copy-start.2 = (bf16[448,1152]{1,0:T(8,128)(2,1)S(1)}, bf16[448,1152]{1,0:T(8,128)(2,1)}, u32[]{:S(2)}) copy-start(bf16[448,1152]{1,0:T(8,128)(2,1)} %param.5) | copy-start | bytes 3096580
  2.6 24.2 %all-to-all-start = ((f32[16,16,1152]{2,1,0:T(8,128)}), f32[16,16,1152]{2,1,0:T(8,128)}, u32[]{:S(2)}, u32[]{:S(2)}) async-start(f32[16,16,1152]{2,1,0:T(8,128)} %shard_map.67), calls=%async_computation | async-start | bytes 2359296 | tf_op jit(solution)/shard_map/all_to_all | solution.py:49
  30.1 1.6 %collective-permute-start = (f32[448,128]{1,0:T(8,128)S(1)}, f32[448,128]{1,0:T(8,128)S(1)}, u32[]{:S(2)}, u32[]{:S(2)}) collective-permute-start(f32[448,128]{1,0:T(8,128)S(1)} %slice_select_fusion), channel_id=1, source_target_pairs={{0,1},{1,0},{2,3},{3,2},{4,5},{5,4},{6,7},{7,6},{8,9},{9,8},{10,11... | collective-permute-start | bytes 688136 | tf_op jit(solution)/shard_map/ppermute | solution.py:63
  64.2 1.5 %collective-permute-start.1 = (f32[448,128]{1,0:T(8,128)S(1)}, f32[448,128]{1,0:T(8,128)S(1)}, u32[]{:S(2)}, u32[]{:S(2)}) collective-permute-start(f32[448,128]{1,0:T(8,128)S(1)} %bitcast.14), channel_id=1, source_target_pairs={{0,1},{1,0},{2,3},{3,2},{4,5},{5,4},{6,7},{7,6},{8,9},{9,8},{10,11... | collective-permute-start | bytes 688136 | tf_op jit(solution)/shard_map/ppermute | solution.py:68
  97.1 23.7 %all-to-all-start.4 = ((f32[16,16,1152]{2,1,0:T(8,128)}), f32[16,16,1152]{2,1,0:T(8,128)S(1)}, u32[]{:S(2)}, u32[]{:S(2)}) async-start(f32[16,16,1152]{2,1,0:T(8,128)} %get-tuple-element.14), calls=%async_computation.4 | async-start | bytes 2359296 | tf_op jit(solution)/shard_map/all_to_all | solution.py:49
  103.0 3.8 %collective-permute-start.2 = (f32[16,384]{1,0:T(8,128)S(1)}, f32[16,384]{1,0:T(8,128)S(1)}, u32[]{:S(2)}, u32[]{:S(2)}) collective-permute-start(f32[16,384]{1,0:T(8,128)S(1)} %get-tuple-element.13), channel_id=1, source_target_pairs={{0,2},{1,3},{2,0},{3,1},{4,6},{5,7},{6,4},{7,5},{8,10},{9,11},{10,... | collective-permute-start | bytes 73736 | tf_op jit(solution)/shard_map/ppermute | solution.py:86
  106.8 5.3 %collective-permute-start.3 = (f32[32,384]{1,0:T(8,128)S(1)}, f32[32,384]{1,0:T(8,128)S(1)}, u32[]{:S(2)}, u32[]{:S(2)}) collective-permute-start(f32[32,384]{1,0:T(8,128)S(1)} %maximum_select_fusion.6), channel_id=1, source_target_pairs={{0,14},{1,15},{2,4},{3,5},{4,2},{5,3},{6,8},{7,9},{8,6},{9,7},{10,... | collective-permute-start | bytes 147464 | tf_op jit(solution)/shard_map/ppermute | solution.py:88
  112.1 1.6 %collective-permute-start.4 = (f32[64,384]{1,0:T(8,128)S(1)}, f32[64,384]{1,0:T(8,128)S(1)}, u32[]{:S(2)}, u32[]{:S(2)}) collective-permute-start(f32[64,384]{1,0:T(8,128)S(1)} %maximum_select_fusion.2), channel_id=1, source_target_pairs={{0,1},{1,0},{2,3},{3,2},{4,5},{5,4},{6,7},{7,6},{8,9},{9,8},{10,11... | collective-permute-start | bytes 294920 | tf_op jit(solution)/shard_map/ppermute | solution.py:89
  122.2 1.2 collective-permute-start.5
  124.1 11.0 %all-to-all-start.5 = ((f32[8,1,256]{2,1,0:T(1,128)}), f32[8,1,256]{2,1,0:T(1,128)S(1)}, u32[]{:S(2)}, u32[]{:S(2)}) async-start(f32[8,1,256]{2,1,0:T(1,128)} %broadcast_in_dim.11), calls=%async_computation.5 | async-start | bytes 16384 | tf_op jit(solution)/shard_map/all_to_all | solution.py:95
  135.1 1.6 %copy-start.3 = (f32[448,1152]{1,0:T(8,128)S(1)}, f32[448,1152]{1,0:T(8,128)}, u32[]{:S(2)}) copy-start(f32[448,1152]{1,0:T(8,128)} %param.6) | copy-start | bytes 6193156
